TPU v7x, 32 devices: a whole 2x2x4 slice. The times are simulated.
32 devices in a mesh: rows: 2 (over x), chan: 16 (over z, y, core).
Axes of the slice: x: 2, y: 2, z: 4, core: 2. Of those that a mesh axis runs over, the one named last changes fastest.
Arguments:
- activations: bfloat16 [64, 7, 7, 512], P('rows', None, None, 'chan'), may hold values from 0 to 2
- cotangents: bfloat16 [64, 512, 49], P('rows', 'chan'), may hold values from -0.0005859375 to 0.0005859375
- ordering: int32 [2, 32], P('rows'), may hold values from 0 to 31, each once within a row
- ridge: float32 [32], replicated, may hold values from 0.2 to 2
Outputs:
- gram_panel: float32 [64, 32], P('rows')
- factor_panel: float32 [64, 32], P('rows')
Inputs may be any that keep to these rules, and one draw needn't show every extreme that they name: Each row of ordering lists every one of the group's 32 examples once.
All inputs are finite; a program needn't handle non-finite values.
Results may differ from a plain program's by a relative error of at most 0.0003.
Values may be sent and summed in bfloat16 or wider, within the bound.
No kernel may reach another device: no remote copies, remote signals or barrier semaphores. Data moves between devices by JAX's collectives and lax.ppermute only.
A program may use at most 64 MiB of HBM per device.

v0:
```python
import jax
import jax.numpy as jnp
from jax import lax
from jax.sharding import PartitionSpec as P

PIV_DEV = 16


def jacobian_block(grad_rows, input_rows):
    example_count = input_rows.shape[0]
    side_len = input_rows.shape[1]
    channel_count = input_rows.shape[3]
    grad_count = grad_rows.shape[1]
    grid_grads = grad_rows.reshape(example_count, grad_count, side_len, side_len)
    padded_grads = jnp.pad(grid_grads, ((0, 0), (0, 0), (1, 1), (1, 1)))
    shifted = []
    for row_shift in range(3):
        for col_shift in range(3):
            window = padded_grads[
                :,
                :,
                2 - row_shift : 2 - row_shift + side_len,
                2 - col_shift : 2 - col_shift + side_len,
            ]
            shifted.append(window.reshape(example_count, grad_count, side_len * side_len))
    stacked_grads = jnp.stack(shifted, axis=2).reshape(
        example_count, grad_count * 9, side_len * side_len
    )
    flat_inputs = input_rows.reshape(example_count, side_len * side_len, channel_count)
    product = jnp.einsum(
        "nkp,npq->nkq", stacked_grads, flat_inputs, preferred_element_type=jnp.float32
    )
    return product.astype(jnp.bfloat16).reshape(example_count, -1)


def gram_block(left_rows, right_rows):
    return lax.dot_general(
        left_rows, right_rows, (((1,), (1,)), ((), ())), preferred_element_type=jnp.float32
    )


def local(activations, cotangents, ordering, ridge):
    local_order = ordering[0]
    own_inputs = jnp.take(activations, local_order, axis=0)
    own_grads = jnp.take(cotangents, local_order, axis=0)
    pivot_count = PIV_DEV
    pivot_inputs, pivot_grads = (
        lax.all_gather(own_inputs[:pivot_count], "rows", axis=0, tiled=True),
        lax.all_gather(own_grads[:pivot_count], "rows", axis=0, tiled=True),
    )
    full_own, full_pivot = (
        lax.all_gather(own_inputs, "chan", axis=3, tiled=True),
        lax.all_gather(pivot_inputs, "chan", axis=3, tiled=True),
    )
    own_jac = jacobian_block(own_grads, full_own)
    pivot_jac = jacobian_block(pivot_grads, full_pivot)
    partial_panel = gram_block(own_jac, pivot_jac)
    gram_panel = lax.psum(partial_panel, "chan")
    diag_block = lax.all_gather(gram_panel[:pivot_count], "rows", axis=0, tiled=True)
    system = 0.5 * (diag_block + diag_block.T) + jnp.diag(ridge)
    lower = jnp.linalg.cholesky(system)
    factor_panel = jax.scipy.linalg.solve_triangular(lower, gram_panel.T, lower=True).T
    return (gram_panel, factor_panel)


def solution(mesh):
    return jax.shard_map(
        local,
        mesh=mesh,
        in_specs=(P("rows", None, None, "chan"), P("rows", "chan", None), P("rows", None), P()),
        out_specs=(P("rows", None), P("rows", None)),
        check_vma=False,
    )
```

profile of v0, /device:TPU:0, one launch (start us, length us, event | category | flops | bytes accessed | tf_op | source)
XLA Modules:
  0.0 280.7 jit_solution(5805800938159762741)
XLA Ops:
  8.6 2.1 gather_fusion.1
  10.9 8.6 %all_gather.17 = bf16[32,7,7,32]{3,0,2,1:T(8,128)(2,1)S(1)} all-gather(bf16[16,7,7,32]{3,0,2,1:T(8,128)(2,1)S(1)} %slice.96), channel_id=1, replica_groups=mesh['rows'=2,'chan'=16] {'rows'}, dimensions={0}, use_global_device_ids=true | all-gather | bytes 150528 | tf_op jit(solution)/shard_map/all_gather | solution.py:48
  19.5 1.0 copy.93
  20.5 1.0 copy.86
  23.1 5.8 %all_gather.16 = bf16[32,32,49]{2,1,0:T(8,128)(2,1)S(1)} all-gather(bf16[16,32,49]{2,1,0:T(8,128)(2,1)S(1)} %slice_select_fusion), channel_id=1, replica_groups=mesh['rows'=2,'chan'=16] {'rows'}, dimensions={0}, use_global_device_ids=true | all-gather | bytes 150528 | tf_op jit(solution)/shard_map/all_gather | solution.py:49
  29.8 1.4 pad_slice_fusion.8
  31.2 2.2 copy.84
  33.4 2.2 copy.78
  35.6 1.2 copy.79
  38.9 1.2 copy.77
  42.1 1.0 constant_dynamic-update-slice_fusion.5
  43.5 2.3 copy.85
  53.4 4.8 %copy.92 = bf16[32,32,9,49]{3,0,2,1:T(8,128)(2,1)S(1)} copy(bf16[32,32,9,49]{1,0,3,2:T(8,128)(2,1)} %bitcast_dynamic-update-slice_fusion) | data formatting | bytes 1806336 | tf_op jit(solution)/shard_map/stack | solution.py:26
  58.2 32.2 %all-gather.5.cloned.1.call-done = bf16[32,7,7,512]{0,2,1,3:T(8,128)(2,1)} async-done(((bf16[32,7,7,32]{0,2,1,3:T(8,128)(2,1)}), bf16[32,7,7,512]{0,2,1,3:T(8,128)(2,1)}) %all-gather.5.cloned.1.call-update) | async-done | bytes 1605648 | tf_op jit(solution)/shard_map/all_gather | solution.py:53
  90.4 8.2 %copy.94 = bf16[32,7,7,512]{3,0,2,1:T(8,128)(2,1)} copy(bf16[32,7,7,512]{0,2,1,3:T(8,128)(2,1)} %all-gather.5.cloned.1.call-done) | data formatting | bytes 3211264 | tf_op jit(solution)/shard_map/all_gather | solution.py:53
  98.7 9.9 %convolution_convert_fusion = bf16[32,288,512]{2,1,0:T(8,128)(2,1)} fusion(bf16[32,288,49]{2,0,1:T(8,128)(2,1)S(1)} %bitcast.70, bf16[32,49,512]{2,0,1:T(8,128)(2,1)} %bitcast.71), kind=kOutput, calls=%fused_computation.5 | convolution fusion | flops 467140608 | bytes 11945984 | tf_op jit(solution)/shard_map/nkp,npq->nkq/dot_general | solution.py:30
  108.6 50.9 %all-gather.3.cloned.1.call-done = bf16[32,7,7,512]{0,2,1,3:T(8,128)(2,1)} async-done(((bf16[32,7,7,32]{0,2,1,3:T(8,128)(2,1)}), bf16[32,7,7,512]{0,2,1,3:T(8,128)(2,1)}) %all-gather.3.cloned.1.call-update) | async-done | bytes 1605648 | tf_op jit(solution)/shard_map/all_gather | solution.py:52
  159.5 8.6 %copy.87 = bf16[32,7,7,512]{3,0,2,1:T(8,128)(2,1)} copy(bf16[32,7,7,512]{0,2,1,3:T(8,128)(2,1)} %all-gather.3.cloned.1.call-done) | data formatting | bytes 3211264 | tf_op jit(solution)/shard_map/all_gather | solution.py:52
  168.1 11.0 %convolution_convert_fusion.1 = bf16[32,288,512]{2,1,0:T(8,128)(2,1)} fusion(bf16[32,288,49]{2,0,1:T(8,128)(2,1)} %bitcast.69, bf16[32,49,512]{2,0,1:T(8,128)(2,1)} %bitcast.72), kind=kOutput, calls=%fused_computation.6 | convolution fusion | flops 467140608 | bytes 11945984 | tf_op jit(solution)/shard_map/nkp,npq->nkq/dot_general | solution.py:30
  179.1 23.4 %fusion.7 = f32[32,32]{1,0:T(8,128)S(1)} fusion(bf16[32,288,512]{2,1,0:T(8,128)(2,1)S(1)} %copy-done.1, bf16[32,288,512]{2,1,0:T(8,128)(2,1)} %convolution_convert_fusion.1), kind=kOutput, calls=%fused_computation.11 | convolution fusion | flops 301989888 | bytes 18878464 | tf_op jit(solution)/shard_map/dot_general | solution.py:37
  202.4 59.2 %psum.7 = f32[32,32]{1,0:T(8,128)S(1)} all-reduce(f32[32,32]{1,0:T(8,128)S(1)} %fusion.7), channel_id=1, replica_groups=mesh['rows'=2,'chan'=16] {'chan'}, use_global_device_ids=true, to_apply=%region_0.1 | all-reduce | flops 1024 | bytes 8192 | tf_op jit(solution)/shard_map/psum | solution.py:58
  261.6 4.4 %all_gather.19 = f32[32,32]{1,0:T(8,128)S(1)} all-gather(f32[16,32]{1,0:T(8,128)S(1)} %slice.97), channel_id=1, replica_groups=mesh['rows'=2,'chan'=16] {'rows'}, dimensions={0}, use_global_device_ids=true | all-gather | bytes 6144 | tf_op jit(solution)/shard_map/all_gather | solution.py:59
  266.2 2.9 %cholesky.16 = f32[32,32]{1,0:T(8,128)S(1)} custom-call(f32[32,32]{1,0:T(8,128)S(1)} %fusion.16), custom_call_target="Cholesky" | custom-call | tf_op jit(solution)/shard_map/jit(cholesky)/cholesky | solution.py:61
  270.4 2.4 custom-call.7
  (57 shorter events, 18.2 us)
Async XLA Ops:
  7.2 1.4 copy-start
  7.2 83.3 %all-gather.5.cloned.1.call-start = ((), (), s32[]{:S(2)}) async-start(), calls=%async_computation.1 | async-start | bytes 7798784 | tf_op jit(solution)/shard_map/all_gather | solution.py:53
  10.7 10.9 %copy-start.3 = (bf16[32,32,49]{2,1,0:T(8,128)(2,1)S(1)}, bf16[32,32,49]{2,1,0:T(8,128)(2,1)}, u32[]{:S(2)}) copy-start(bf16[32,32,49]{2,1,0:T(8,128)(2,1)} %param.5) | copy-start | bytes 301060
  20.5 139.0 %all-gather.3.cloned.1.call-start = ((), (), s32[]{:S(2)}) async-start(), calls=%async_computation | async-start | bytes 7798784 | tf_op jit(solution)/shard_map/all_gather | solution.py:52
  38.9 4.5 %copy-start.2 = (bf16[32,32,1,49]{3,1,0,2:T(8,128)(2,1)S(1)}, bf16[32,32,1,49]{3,1,0,2:T(8,128)(2,1)}, u32[]{:S(2)}) copy-start(bf16[32,32,1,49]{3,1,0,2:T(8,128)(2,1)} %copy.84) | copy-start | bytes 301060
  168.1 11.0 %copy-start.1 = (bf16[32,288,512]{2,1,0:T(8,128)(2,1)S(1)}, bf16[32,288,512]{2,1,0:T(8,128)(2,1)}, u32[]{:S(2)}) copy-start(bf16[32,288,512]{2,1,0:T(8,128)(2,1)} %convolution_convert_fusion) | copy-start | bytes 28311556
  179.1 87.0 %copy-start.5 = (f32[32]{0:T(128)S(1)}, f32[32]{0:T(128)}, u32[]{:S(2)}) copy-start(f32[32]{0:T(128)} %param.7) | copy-start | bytes 388
  261.6 12.1 %copy-start.4 = (f32[32,32]{1,0:T(8,128)}, f32[32,32]{1,0:T(8,128)S(1)}, u32[]{:S(2)}) copy-start(f32[32,32]{1,0:T(8,128)S(1)} %psum.7) | copy-start | bytes 12292
Sparse Core Ops, SparseCore 0:
  20.6 69.7 all-gather.4
  92.7 66.6 all-gather.2
where the time goes:
time: 284 us; the launch traced here: 281 us
  waiting for transfers between devices  83.1 us (29%)
  blocking collectives  77.9 us (27%)
  local copies, waits for them, and re-layouts  51.5 us (18%)
  matrix products  45 us (16%)
  between operations  14.4 us (5%)
  other arithmetic  8.59 us (3%)
    psum x1, blocking collectives, local(): gram_panel = lax.psum(partial_panel, 'chan')  59.2 us
    all_gather x1, waiting for transfers between devices, local(): lax.all_gather(own_inputs, 'chan', axis=3, tiled=True)  50.9 us
    all_gather x1, waiting for transfers between devices, local(): lax.all_gather(pivot_inputs, 'chan', axis=3, tiled=True)  32.2 us
    dot_general x1, matrix products, gram_block(): lax.dot_general(left_rows, right_rows, (((1,), (1,)), ((), ())), preferre...  23.4 us
    dot_general x2, matrix products, jacobian_block(): jnp.einsum('nkp,npq->nkq', stacked_grads, flat_inputs, preferred_element_...  20.9 us
    another operation x12, local copies, waits for them, and re-layouts, jacobian_block(): jnp.stack(shifted, axis=2)  16.9 us
    unnamed x27, local copies, waits for them, and re-layouts  9.41 us
    all_gather x1, local copies, waits for them, and re-layouts, local(): lax.all_gather(own_inputs, 'chan', axis=3, tiled=True)  8.62 us
  transfers between devices with their start and end apart: 2, of which 2 were waited for; matrix products, arithmetic and copies ran while one was open for 18% of the time, Pallas kernels for 0%

commit v1 on v0

--- a/solution.py
+++ b/solution.py
@@ -1,9 +1,243 @@
+import functools
+
 import jax
 import jax.numpy as jnp
 from jax import lax
+from jax.experimental import pallas as pl
+from jax.experimental.pallas import tpu as pltpu
 from jax.sharding import PartitionSpec as P
 
 PIV_DEV = 16
+
+SIDE = 7
+PITCH = 8
+GROUPS4 = 14
+CH = 32
+EX = 32
+LANES = 128
+F32 = jnp.float32
+BF16 = jnp.bfloat16
+
+
+def prep_kernel(order_ref, x_ref, g_ref, xo_ref, go_ref, xp_ref, gp_ref, gs, gt, gout):
+    row_id = lax.broadcasted_iota(jnp.int32, (EX, EX), 0)
+    col_id = lax.broadcasted_iota(jnp.int32, (EX, EX), 1)
+    onehot = jnp.zeros((EX, EX), F32)
+    for k in range(EX):
+        example = order_ref[0, k]
+        onehot = jnp.where((row_id == k) & (col_id == example), 1.0, onehot)
+        gs[k * CH:(k + 1) * CH, 0:SIDE * SIDE] = g_ref[example].astype(F32)
+    onehot = onehot.astype(BF16)
+    zero_block = jnp.zeros((EX, CH), BF16)
+    for group in range(GROUPS4):
+        pieces = []
+        for j in range(4):
+            py, px = group // 2, (group % 2) * 4 + j
+            pieces.append(x_ref[py * SIDE + px] if px < SIDE else zero_block)
+        packed = jnp.concatenate(pieces, axis=1)
+        ordered = jnp.dot(onehot, packed, preferred_element_type=F32).astype(BF16)
+        xo_ref[group] = ordered
+        xp_ref[group] = ordered[:PIV_DEV]
+    block_id = lax.broadcasted_iota(jnp.int32, (GROUPS4, LANES), 1) // CH
+    for quad in range(EX // 4):
+        flipped = jnp.transpose(gs[quad * LANES:(quad + 1) * LANES, :])
+        for py in range(SIDE):
+            gt[py * PITCH:py * PITCH + SIDE, :] = flipped[py * SIDE:(py + 1) * SIDE, :]
+            gt[py * PITCH + SIDE:(py + 1) * PITCH, :] = jnp.zeros((1, LANES), F32)
+        parts = [gt[pl.ds(j, GROUPS4, stride=4), :] for j in range(4)]
+        for e in range(4):
+            merged = jnp.zeros((GROUPS4, LANES), F32)
+            for j in range(4):
+                shift = (CH * (j - e)) % LANES
+                moved = pltpu.roll(parts[j], shift, 1) if shift else parts[j]
+                merged = jnp.where(block_id == j, moved, merged)
+            gout[pl.ds(quad * 4 + e, GROUPS4, stride=EX), :] = merged
+    for group in range(GROUPS4):
+        ordered = gout[group * EX:(group + 1) * EX, :].astype(BF16)
+        go_ref[group] = ordered
+        gp_ref[group] = ordered[:PIV_DEV]
+
+
+def prep(order, x, g):
+    full = jax.ShapeDtypeStruct((GROUPS4, EX, LANES), BF16)
+    part = jax.ShapeDtypeStruct((GROUPS4, PIV_DEV, LANES), BF16)
+    vmem = pl.BlockSpec(memory_space=pltpu.VMEM)
+    return pl.pallas_call(
+        prep_kernel,
+        out_shape=(full, full, part, part),
+        in_specs=[pl.BlockSpec(memory_space=pltpu.SMEM), vmem, vmem],
+        out_specs=(vmem,) * 4,
+        scratch_shapes=[
+            pltpu.VMEM((EX * CH, LANES), F32),
+            pltpu.VMEM((SIDE * PITCH, LANES), F32),
+            pltpu.VMEM((GROUPS4 * EX, LANES), F32),
+        ],
+        compiler_params=pltpu.CompilerParams(vmem_limit_bytes=16 << 20),
+        name="prep",
+    )(order, x, g)
+
+
+def unpack(refs, group):
+    values = [ref[group] for ref in refs]
+    return [
+        jnp.concatenate([v[:, j * CH:(j + 1) * CH] for v in values], axis=1)
+        for j in range(4)
+    ]
+
+
+ROWB = SIDE * EX
+COLB = PITCH * EX
+
+
+def main_kernel(*refs):
+    xo, xc, go, gc = refs[0:4], refs[4:8], refs[8:12], refs[12:16]
+    out_ref, lx, rx, lg, rg, t = refs[16:]
+    zero_rows = jnp.zeros((EX, LANES), BF16)
+    for py in range(SIDE):
+        first, last = py * ROWB, py * ROWB + ROWB - EX
+        lx[first:first + EX, 0:LANES] = zero_rows
+        lx[last:last + EX, 2 * LANES:3 * LANES] = zero_rows
+        first, last = py * COLB, py * COLB + COLB - EX
+        rx[first:first + EX, 0:LANES] = zero_rows
+        rx[last - EX:last, 2 * LANES:3 * LANES] = zero_rows
+        for d in range(3):
+            rx[last:last + EX, d * LANES:(d + 1) * LANES] = zero_rows
+        rg[last:last + EX, :] = zero_rows
+    for group in range(GROUPS4):
+        own_x, other_x = unpack(xo, group), unpack(xc, group)
+        own_g, other_g = unpack(go, group), unpack(gc, group)
+        for j in range(4):
+            py, px = group // 2, (group % 2) * 4 + j
+            if px == SIDE:
+                continue
+            row, col = (py * SIDE + px) * EX, (py * PITCH + px) * EX
+            piv_x = jnp.concatenate([own_x[j][:PIV_DEV], other_x[j]], axis=0)
+            for d in (-1, 0, 1):
+                if 0 <= px - d < SIDE:
+                    lanes = slice((d + 1) * LANES, (d + 2) * LANES)
+                    lx[row - d * EX:row - d * EX + EX, lanes] = own_x[j]
+                    rx[col - d * EX:col - d * EX + EX, lanes] = piv_x
+            lg[row:row + EX, :] = own_g[j]
+            rg[col:col + EX, :] = jnp.concatenate([own_g[j][:PIV_DEV], other_g[j]], axis=0)
+
+    contract = (((1,), (1,)), ((), ()))
+    for qy in range(SIDE):
+        right = rx[qy * COLB:(qy + 1) * COLB, :]
+        for py in range(SIDE):
+            left = lx[py * ROWB:(py + 1) * ROWB, :]
+            t[py * SIDE + qy] = lax.dot_general(left, right, contract, preferred_element_type=F32)
+    acc = jnp.zeros((EX, COLB), F32)
+    for qy in range(SIDE):
+        right = rg[qy * COLB:(qy + 1) * COLB, :]
+        for py in range(SIDE):
+            left = lg[py * ROWB:(py + 1) * ROWB, :]
+            gg = lax.dot_general(left, right, contract, preferred_element_type=F32)
+            for px in range(SIDE):
+                rows = slice(px * EX, (px + 1) * EX)
+                total = t[py * SIDE + qy, rows, :]
+                if py > 0 and qy > 0:
+                    total = total + t[(py - 1) * SIDE + qy - 1, rows, :]
+                if py < SIDE - 1 and qy < SIDE - 1:
+                    total = total + t[(py + 1) * SIDE + qy + 1, rows, :]
+                acc = acc + gg[rows, :] * total
+    folded = acc[:, :LANES] + acc[:, LANES:]
+    folded = folded + pltpu.roll(folded, 64, 1)
+    folded = folded + pltpu.roll(folded, 32, 1)
+    folded = jnp.where(lax.axis_index("rows") == 1, pltpu.roll(folded, 16, 1), folded)
+    block_id = lax.broadcasted_iota(jnp.int32, (8, LANES), 1) // EX
+    packed = folded[0:8]
+    for j in range(1, 4):
+        packed = jnp.where(block_id == j, folded[8 * j:8 * j + 8], packed)
+    out_ref[...] = packed
+
+
+def main(arrays):
+    vmem = pl.BlockSpec(memory_space=pltpu.VMEM)
+    rows, cols = SIDE * ROWB, SIDE * COLB
+    return pl.pallas_call(
+        main_kernel,
+        out_shape=jax.ShapeDtypeStruct((8, LANES), F32),
+        in_specs=[vmem] * 16,
+        out_specs=vmem,
+        scratch_shapes=[
+            pltpu.VMEM((rows, 3 * LANES), BF16),
+            pltpu.VMEM((cols, 3 * LANES), BF16),
+            pltpu.VMEM((rows, LANES), BF16),
+            pltpu.VMEM((cols, LANES), BF16),
+            pltpu.VMEM((SIDE * SIDE, ROWB, COLB), F32),
+        ],
+        compiler_params=pltpu.CompilerParams(vmem_limit_bytes=40 << 20),
+        name="terms",
+    )(*arrays)
+
+
+def rows_of(packed, count):
+    return jnp.concatenate(
+        [packed[:, EX * j:EX * (j + 1)] for j in range(count)], axis=0
+    )
+
+
+def final_kernel(*refs):
+    own, other = refs[0:4], refs[4:8]
+    ridge_ref, gram_ref, factor_ref = refs[8:]
+    panel = rows_of((own[0][...] + own[1][...]) + (own[2][...] + own[3][...]), 4)
+    cross = rows_of((other[0][...] + other[1][...]) + (other[2][...] + other[3][...]), 2)
+    gram_ref[...] = panel
+    first = lax.axis_index("rows") == 0
+    mine = panel[:PIV_DEV]
+    diag = jnp.concatenate([jnp.where(first, mine, cross), jnp.where(first, cross, mine)], axis=0)
+    row_id = lax.broadcasted_iota(jnp.int32, (EX, EX), 0)
+    col_id = lax.broadcasted_iota(jnp.int32, (EX, EX), 1)
+    ridge = jnp.where(row_id == col_id, jnp.broadcast_to(ridge_ref[...], (EX, EX)), 0.0)
+    system = 0.5 * (diag + jnp.transpose(diag)) + ridge
+    factor = jnp.zeros((EX, EX), F32)
+    for j in range(EX):
+        scale = lax.rsqrt(system[j:j + 1, j:j + 1])
+        line = system[j:j + 1, :] * scale
+        below = system[:, j:j + 1] * scale
+        solved = panel[:, j:j + 1] * scale
+        factor = jnp.where(col_id == j, solved, factor)
+        if j < EX - 1:
+            system = system - below * line
+            panel = panel - solved * line
+    factor_ref[...] = factor
+
+
+def final(own, other, ridge):
+    vmem = pl.BlockSpec(memory_space=pltpu.VMEM)
+    out = jax.ShapeDtypeStruct((EX, EX), F32)
+    return pl.pallas_call(
+        final_kernel,
+        out_shape=(out, out),
+        in_specs=[vmem] * 9,
+        out_specs=(vmem, vmem),
+        name="solve",
+    )(*own, *other, ridge.reshape(1, EX))
+
+
+def exchange(value, count, flip):
+    return lax.ppermute(value, "chan", [(i, i ^ flip) for i in range(count)])
+
+
+def exchange_across(value, count, flip):
+    pairs = [(g * count + i, (1 - g) * count + (i ^ flip)) for g in range(2) for i in range(count)]
+    return lax.ppermute(value, ("rows", "chan"), pairs)
+
+
+def local_packed(count, activations, cotangents, ordering, ridge):
+    near, far = (1, 2, 3), (4, 8, 12)
+    x = jnp.transpose(activations, (1, 2, 0, 3)).reshape(SIDE * SIDE, EX, CH)
+    xo, go, xp, gp = prep(ordering, x, cotangents)
+    own_g = [go] + [exchange(go, count, f) for f in far]
+    other_g = [exchange_across(gp, count, f) for f in (0,) + far]
+    own_x = [xo] + [exchange(xo, count, f) for f in near]
+    other_x = [exchange_across(xp, count, f) for f in (0,) + near]
+    term = main(own_x + other_x + own_g + other_g)
+    terms = [term] + [exchange(term, count, f) for f in near]
+    part = (terms[0] + terms[1]) + (terms[2] + terms[3])
+    own = [part] + [exchange(part, count, f) for f in far]
+    other = [exchange_across(part, count, f) for f in (0,) + far]
+    return final(own, other, ridge)
 
 
 def jacobian_block(grad_rows, input_rows):
@@ -64,8 +298,10 @@
 
 
 def solution(mesh):
+    row_groups, count = mesh.shape["rows"], mesh.shape["chan"]
+    packed = row_groups == 2 and count == 16
     return jax.shard_map(
-        local,
+        functools.partial(local_packed, count) if packed else local,
         mesh=mesh,
         in_specs=(P("rows", None, None, "chan"), P("rows", "chan", None), P("rows", None), P()),
         out_specs=(P("rows", None), P("rows", None)),

time: 284 us -> 63 us (0.22); the launches traced: 281 us -> 62.8 us
  blocking collectives: 77.9 us -> 0 us
  waiting for transfers between devices: 83.1 us -> 14.7 us
  local copies, waits for them, and re-layouts: 51.5 us -> 3.16 us
  matrix products: 45 us -> 0 us
  starting transfers between devices: 0.08 us -> 33.4 us
  between operations: 14.4 us -> 0.76 us
  Pallas kernels: 0 us -> 10.8 us
  other arithmetic: 8.59 us -> 0.01 us
    all_gather x2 -> x0, waiting for transfers between devices: 83.1 us -> none  [the longest x1 50.9 us: local(): lax.all_gather(own_inputs, 'chan', axis=3, tiled=True)]
    psum x1 -> x0, blocking collectives: 59.2 us -> none  [local(): gram_panel = lax.psum(partial_panel, 'chan')]
    dot_general x3 -> x0, matrix products: 44.2 us -> none  [the longest x1 23.4 us: gram_block(): lax.dot_general(left_rows, right_rows, (((1,), (1,)), ((), ())), preferre...]
    ppermute x0 -> x24, starting transfers between devices: none -> 33.4 us  [the longest x12 20.1 us: exchange_across(): return lax.ppermute(value, ('rows', 'chan'), pairs)]
    all_gather x3 -> x0, blocking collectives: 18.8 us -> none  [the longest x1 8.59 us: local(): lax.all_gather(own_inputs[:pivot_count], 'rows', axis=0, tiled=True)]
    all_gather x5 -> x0, local copies, waits for them, and re-layouts: 18.7 us -> none  [the longest x1 8.62 us: local(): lax.all_gather(own_inputs, 'chan', axis=3, tiled=True)]
    another operation x12 -> x0, local copies, waits for them, and re-layouts: 16.9 us -> none  [jacobian_block(): jnp.stack(shifted, axis=2)]
    ppermute x0 -> x24, waiting for transfers between devices: none -> 14.7 us  [the longest x12 12.6 us: exchange(): return lax.ppermute(value, 'chan', [(i, i ^ flip) for i in range(count)])]
  transfers between devices with their start and end apart: 2 -> 24, of which waited for: 2 -> 8; matrix products, arithmetic and copies ran while one was open for 18% -> 0% of each run, Pallas kernels for 0% -> 0%
where the time goes in v1:
time: 63 us; the launch traced here: 62.8 us
  starting transfers between devices  33.4 us (53%)
  waiting for transfers between devices  14.7 us (23%)
  Pallas kernels  10.8 us (17%)
  local copies, waits for them, and re-layouts  3.16 us (5%)
  between operations  0.76 us (1%)
    ppermute x12, starting transfers between devices, exchange_across(): return lax.ppermute(value, ('rows', 'chan'), pairs)  20.1 us
    ppermute x12, starting transfers between devices, exchange(): return lax.ppermute(value, 'chan', [(i, i ^ flip) for i in range(count)])  13.3 us
    ppermute x12, waiting for transfers between devices, exchange(): return lax.ppermute(value, 'chan', [(i, i ^ flip) for i in range(count)])  12.6 us
    pallas_call x1, Pallas kernels, main(): pl.pallas_call(main_kernel, out_shape=jax.ShapeDtypeStruct((8, LANES), F3...  5.59 us
    pallas_call x1, Pallas kernels, final(): pl.pallas_call(final_kernel, out_shape=(out, out), in_specs=[vmem] * 9, o...  4.1 us
    unnamed x22, local copies, waits for them, and re-layouts  3.16 us
    ppermute x12, waiting for transfers between devices, exchange_across(): return lax.ppermute(value, ('rows', 'chan'), pairs)  2.04 us
  transfers between devices with their start and end apart: 24, of which 8 were waited for; matrix products, arithmetic and copies ran while one was open for 0% of the time, Pallas kernels for 0%

profile of v1, /device:TPU:0, one launch (start us, length us, event | category | flops | bytes accessed | tf_op | source)
XLA Modules:
  0.0 62.8 jit_solution(6117795423390744742)
XLA Ops:
  1.3 1.0 %copy-done = bf16[32,7,7,32]{3,0,2,1:T(8,128)(2,1)S(1)} copy-done((bf16[32,7,7,32]{3,0,2,1:T(8,128)(2,1)S(1)}, bf16[32,7,7,32]{3,0,2,1:T(8,128)(2,1)}, u32[]{:S(2)}) %copy-start) | copy-done | bytes 100376
  3.2 1.1 %prep.1 = (bf16[14,32,128]{2,1,0:T(8,128)(2,1)S(1)}, bf16[14,32,128]{2,1,0:T(8,128)(2,1)S(1)}, bf16[14,16,128]{2,1,0:T(8,128)(2,1)S(1)}, bf16[14,16,128]{2,1,0:T(8,128)(2,1)S(1)}) custom-call(s32[1,32]{1,0:T(1,128)S(1)} %copy-done.2, bf16[49,32,32]{2,1,0:T(8,128)(2,1)S(1)} %bitcast.4, bf16[32,32,49]{2,1,0:T(8,128)(2,1)S(1)} %copy-done.1), custom_call_target="tpu_custom_call" | custom-call | tf_op jit(solution)/shard_map/prep/pallas_call | solution.py:65
  4.4 3.4 %collective-permute-start.6 = (bf16[14,16,128]{2,1,0:T(8,128)(2,1)S(1)}, bf16[14,16,128]{2,1,0:T(8,128)(2,1)S(1)}, u32[]{:S(2)}, u32[]{:S(2)}) collective-permute-start(bf16[14,16,128]{2,1,0:T(8,128)(2,1)S(1)} %get-tuple-element.7), channel_id=1, source_target_pairs={{0,19},{1,18},{2,17},{3,16},{4,23},{5,22},{6,21},{7,20},{8,27},{9,... | collective-permute-start | bytes 172040 | tf_op jit(solution)/shard_map/ppermute | solution.py:224
  8.4 1.4 %collective-permute-start.4 = (bf16[14,16,128]{2,1,0:T(8,128)(2,1)S(1)}, bf16[14,16,128]{2,1,0:T(8,128)(2,1)S(1)}, u32[]{:S(2)}, u32[]{:S(2)}) collective-permute-start(bf16[14,16,128]{2,1,0:T(8,128)(2,1)S(1)} %get-tuple-element.7), channel_id=1, source_target_pairs={{0,17},{1,16},{2,19},{3,18},{4,21},{5,20},{6,23},{7,22},{8,25},{9,... | collective-permute-start | bytes 172040 | tf_op jit(solution)/shard_map/ppermute | solution.py:224
  10.1 1.2 %collective-permute-start.2 = (bf16[14,32,128]{2,1,0:T(8,128)(2,1)S(1)}, bf16[14,32,128]{2,1,0:T(8,128)(2,1)S(1)}, u32[]{:S(2)}, u32[]{:S(2)}) collective-permute-start(bf16[14,32,128]{2,1,0:T(8,128)(2,1)S(1)} %get-tuple-element.6.refs_0_), channel_id=1, source_target_pairs={{0,3},{1,2},{2,1},{3,0},{4,7},{5,6},{6,5},{7,4},{8,11},{9,10},{10,... | collective-permute-start | bytes 344072 | tf_op jit(solution)/shard_map/ppermute | solution.py:219
  11.2 4.5 %collective-permute-start.13 = (bf16[14,16,128]{2,1,0:T(8,128)(2,1)S(1)}, bf16[14,16,128]{2,1,0:T(8,128)(2,1)S(1)}, u32[]{:S(2)}, u32[]{:S(2)}) collective-permute-start(bf16[14,16,128]{2,1,0:T(8,128)(2,1)S(1)} %get-tuple-element.9), channel_id=1, source_target_pairs={{0,28},{1,29},{2,30},{3,31},{4,24},{5,25},{6,26},{7,27},{8,20},{9,... | collective-permute-start | bytes 172040 | tf_op jit(solution)/shard_map/ppermute | solution.py:224
  15.8 2.7 %collective-permute-start.11 = (bf16[14,16,128]{2,1,0:T(8,128)(2,1)S(1)}, bf16[14,16,128]{2,1,0:T(8,128)(2,1)S(1)}, u32[]{:S(2)}, u32[]{:S(2)}) collective-permute-start(bf16[14,16,128]{2,1,0:T(8,128)(2,1)S(1)} %get-tuple-element.9), channel_id=1, source_target_pairs={{0,20},{1,21},{2,22},{3,23},{4,16},{5,17},{6,18},{7,19},{8,28},{9,... | collective-permute-start | bytes 172040 | tf_op jit(solution)/shard_map/ppermute | solution.py:224
  18.8 1.5 %collective-permute-start.1 = (bf16[14,32,128]{2,1,0:T(8,128)(2,1)S(1)}, bf16[14,32,128]{2,1,0:T(8,128)(2,1)S(1)}, u32[]{:S(2)}, u32[]{:S(2)}) collective-permute-start(bf16[14,32,128]{2,1,0:T(8,128)(2,1)S(1)} %get-tuple-element.6.refs_0_), channel_id=1, source_target_pairs={{0,2},{1,3},{2,0},{3,1},{4,6},{5,7},{6,4},{7,5},{8,10},{9,11},{10,... | collective-permute-start | bytes 344072 | tf_op jit(solution)/shard_map/ppermute | solution.py:219
  20.3 1.9 %collective-permute-done.12.refs_14_ = bf16[14,16,128]{2,1,0:T(8,128)(2,1)S(1)} collective-permute-done((bf16[14,16,128]{2,1,0:T(8,128)(2,1)S(1)}, bf16[14,16,128]{2,1,0:T(8,128)(2,1)S(1)}, u32[]{:S(2)}, u32[]{:S(2)}) %collective-permute-start.12) | collective-permute-done | bytes 57376 | tf_op jit(solution)/shard_map/ppermute | solution.py:224
  22.3 2.4 %collective-permute-start.9 = (bf16[14,32,128]{2,1,0:T(8,128)(2,1)S(1)}, bf16[14,32,128]{2,1,0:T(8,128)(2,1)S(1)}, u32[]{:S(2)}, u32[]{:S(2)}) collective-permute-start(bf16[14,32,128]{2,1,0:T(8,128)(2,1)S(1)} %get-tuple-element.8.refs_8_), channel_id=1, source_target_pairs={{0,12},{1,13},{2,14},{3,15},{4,8},{5,9},{6,10},{7,11},{8,4},{9,5},... | collective-permute-start | bytes 344072 | tf_op jit(solution)/shard_map/ppermute | solution.py:219
  25.0 1.8 %collective-permute-start.7 = (bf16[14,32,128]{2,1,0:T(8,128)(2,1)S(1)}, bf16[14,32,128]{2,1,0:T(8,128)(2,1)S(1)}, u32[]{:S(2)}, u32[]{:S(2)}) collective-permute-start(bf16[14,32,128]{2,1,0:T(8,128)(2,1)S(1)} %get-tuple-element.8.refs_8_), channel_id=1, source_target_pairs={{0,4},{1,5},{2,6},{3,7},{4,0},{5,1},{6,2},{7,3},{8,12},{9,13},{10,... | collective-permute-start | bytes 344072 | tf_op jit(solution)/shard_map/ppermute | solution.py:219
  26.7 3.5 %collective-permute-done.9.refs_11_ = bf16[14,32,128]{2,1,0:T(8,128)(2,1)S(1)} collective-permute-done((bf16[14,32,128]{2,1,0:T(8,128)(2,1)S(1)}, bf16[14,32,128]{2,1,0:T(8,128)(2,1)S(1)}, u32[]{:S(2)}, u32[]{:S(2)}) %collective-permute-start.9) | collective-permute-done | bytes 114720 | tf_op jit(solution)/shard_map/ppermute | solution.py:219
  30.2 4.3 %collective-permute-done.8.refs_10_ = bf16[14,32,128]{2,1,0:T(8,128)(2,1)S(1)} collective-permute-done((bf16[14,32,128]{2,1,0:T(8,128)(2,1)S(1)}, bf16[14,32,128]{2,1,0:T(8,128)(2,1)S(1)}, u32[]{:S(2)}, u32[]{:S(2)}) %collective-permute-start.8) | collective-permute-done | bytes 114720 | tf_op jit(solution)/shard_map/ppermute | solution.py:219
  34.6 5.6 %terms.1 = f32[8,128]{1,0:T(8,128)S(1)} custom-call(bf16[14,32,128]{2,1,0:T(8,128)(2,1)S(1)} %get-tuple-element.6.refs_0_, bf16[14,32,128]{2,1,0:T(8,128)(2,1)S(1)} %collective-permute-done.refs_1_, bf16[14,32,128]{2,1,0:T(8,128)(2,1)S(1)} %collective-permute-done.1.refs_2_, bf16[14,32,128]{2,1,0:T(8,128)(2,1)S(1)} %collective-permute-done.2.refs_3_, ...), custom_call_target="tpu_custom_call" | custom-call | tf_op jit(solution)/shard_map/terms/pallas_call | solution.py:157
  42.0 1.2 %collective-permute-done.16 = f32[8,128]{1,0:T(8,128)S(1)} collective-permute-done((f32[8,128]{1,0:T(8,128)S(1)}, f32[8,128]{1,0:T(8,128)S(1)}, u32[]{:S(2)}, u32[]{:S(2)}) %collective-permute-start.16) | collective-permute-done | bytes 4128 | tf_op jit(solution)/shard_map/ppermute | solution.py:219
  43.2 1.3 %collective-permute-done.15 = f32[8,128]{1,0:T(8,128)S(1)} collective-permute-done((f32[8,128]{1,0:T(8,128)S(1)}, f32[8,128]{1,0:T(8,128)S(1)}, u32[]{:S(2)}, u32[]{:S(2)}) %collective-permute-start.15) | collective-permute-done | bytes 4128 | tf_op jit(solution)/shard_map/ppermute | solution.py:219
  44.5 2.7 %collective-permute-start.23 = (f32[8,128]{1,0:T(8,128)S(1)}, f32[8,128]{1,0:T(8,128)S(1)}, u32[]{:S(2)}, u32[]{:S(2)}) collective-permute-start(f32[8,128]{1,0:T(8,128)S(1)} %add_add_fusion.refs_0_), channel_id=1, source_target_pairs={{0,28},{1,29},{2,30},{3,31},{4,24},{5,25},{6,26},{7,27},{8,20},{9,... | collective-permute-start | bytes 12296 | tf_op jit(solution)/shard_map/ppermute | solution.py:224
  47.2 2.8 %collective-permute-start.21 = (f32[8,128]{1,0:T(8,128)S(1)}, f32[8,128]{1,0:T(8,128)S(1)}, u32[]{:S(2)}, u32[]{:S(2)}) collective-permute-start(f32[8,128]{1,0:T(8,128)S(1)} %add_add_fusion.refs_0_), channel_id=1, source_target_pairs={{0,20},{1,21},{2,22},{3,23},{4,16},{5,17},{6,18},{7,19},{8,28},{9,... | collective-permute-start | bytes 12296 | tf_op jit(solution)/shard_map/ppermute | solution.py:224
  50.1 1.2 %collective-permute-start.20 = (f32[8,128]{1,0:T(8,128)S(1)}, f32[8,128]{1,0:T(8,128)S(1)}, u32[]{:S(2)}, u32[]{:S(2)}) collective-permute-start(f32[8,128]{1,0:T(8,128)S(1)} %add_add_fusion.refs_0_), channel_id=1, source_target_pairs={{0,16},{1,17},{2,18},{3,19},{4,20},{5,21},{6,22},{7,23},{8,24},{9,... | collective-permute-start | bytes 12296 | tf_op jit(solution)/shard_map/ppermute | solution.py:224
  51.3 2.2 %collective-permute-start.19 = (f32[8,128]{1,0:T(8,128)S(1)}, f32[8,128]{1,0:T(8,128)S(1)}, u32[]{:S(2)}, u32[]{:S(2)}) collective-permute-start(f32[8,128]{1,0:T(8,128)S(1)} %add_add_fusion.refs_0_), channel_id=1, source_target_pairs={{0,12},{1,13},{2,14},{3,15},{4,8},{5,9},{6,10},{7,11},{8,4},{9,5},... | collective-permute-start | bytes 12296 | tf_op jit(solution)/shard_map/ppermute | solution.py:219
  53.6 2.1 %collective-permute-start.17 = (f32[8,128]{1,0:T(8,128)S(1)}, f32[8,128]{1,0:T(8,128)S(1)}, u32[]{:S(2)}, u32[]{:S(2)}) collective-permute-start(f32[8,128]{1,0:T(8,128)S(1)} %add_add_fusion.refs_0_), channel_id=1, source_target_pairs={{0,4},{1,5},{2,6},{3,7},{4,0},{5,1},{6,2},{7,3},{8,12},{9,13},{10,... | collective-permute-start | bytes 12296 | tf_op jit(solution)/shard_map/ppermute | solution.py:219
  55.8 1.0 %collective-permute-done.19.refs_3_ = f32[8,128]{1,0:T(8,128)S(1)} collective-permute-done((f32[8,128]{1,0:T(8,128)S(1)}, f32[8,128]{1,0:T(8,128)S(1)}, u32[]{:S(2)}, u32[]{:S(2)}) %collective-permute-start.19) | collective-permute-done | bytes 4128 | tf_op jit(solution)/shard_map/ppermute | solution.py:219
  56.7 1.3 %collective-permute-done.18.refs_2_ = f32[8,128]{1,0:T(8,128)S(1)} collective-permute-done((f32[8,128]{1,0:T(8,128)S(1)}, f32[8,128]{1,0:T(8,128)S(1)}, u32[]{:S(2)}, u32[]{:S(2)}) %collective-permute-start.18) | collective-permute-done | bytes 4128 | tf_op jit(solution)/shard_map/ppermute | solution.py:219
  58.7 4.1 %solve.1 = (f32[32,32]{1,0:T(8,128)}, f32[32,32]{1,0:T(8,128)}) custom-call(f32[8,128]{1,0:T(8,128)} %copy-done.3, f32[8,128]{1,0:T(8,128)} %copy-done.10, f32[8,128]{1,0:T(8,128)} %copy-done.9, f32[8,128]{1,0:T(8,128)} %copy-done.8, f32[8,128]{1,0:T(8,128)} %copy-done.7, f32[8,128]{1,0:T(8,128)} %copy-done.6, f32[8,128]{1,0:T(8,128)} %copy-done.5, ...), custom_call_target="tpu_custom_call" | custom-call | tf_op jit(solution)/shard_map/solve/pallas_call | solution.py:209
  (50 shorter events, 5.7 us)
Async XLA Ops:
  4.4 6.9 %collective-permute-start.6 = (bf16[14,16,128]{2,1,0:T(8,128)(2,1)S(1)}, bf16[14,16,128]{2,1,0:T(8,128)(2,1)S(1)}, u32[]{:S(2)}, u32[]{:S(2)}) collective-permute-start(bf16[14,16,128]{2,1,0:T(8,128)(2,1)S(1)} %get-tuple-element.7), channel_id=1, source_target_pairs={{0,19},{1,18},{2,17},{3,16},{4,23},{5,22},{6,21},{7,20},{8,27},{9,... | collective-permute-start | bytes 172040 | tf_op jit(solution)/shard_map/ppermute | solution.py:224
  7.8 8.0 %collective-permute-start.5 = (bf16[14,16,128]{2,1,0:T(8,128)(2,1)S(1)}, bf16[14,16,128]{2,1,0:T(8,128)(2,1)S(1)}, u32[]{:S(2)}, u32[]{:S(2)}) collective-permute-start(bf16[14,16,128]{2,1,0:T(8,128)(2,1)S(1)} %get-tuple-element.7), channel_id=1, source_target_pairs={{0,18},{1,19},{2,16},{3,17},{4,22},{5,23},{6,20},{7,21},{8,26},{9,... | collective-permute-start | bytes 172040 | tf_op jit(solution)/shard_map/ppermute | solution.py:224
  8.4 7.4 %collective-permute-start.4 = (bf16[14,16,128]{2,1,0:T(8,128)(2,1)S(1)}, bf16[14,16,128]{2,1,0:T(8,128)(2,1)S(1)}, u32[]{:S(2)}, u32[]{:S(2)}) collective-permute-start(bf16[14,16,128]{2,1,0:T(8,128)(2,1)S(1)} %get-tuple-element.7), channel_id=1, source_target_pairs={{0,17},{1,16},{2,19},{3,18},{4,21},{5,20},{6,23},{7,22},{8,25},{9,... | collective-permute-start | bytes 172040 | tf_op jit(solution)/shard_map/ppermute | solution.py:224
  9.8 8.8 %collective-permute-start.3 = (bf16[14,16,128]{2,1,0:T(8,128)(2,1)S(1)}, bf16[14,16,128]{2,1,0:T(8,128)(2,1)S(1)}, u32[]{:S(2)}, u32[]{:S(2)}) collective-permute-start(bf16[14,16,128]{2,1,0:T(8,128)(2,1)S(1)} %get-tuple-element.7), channel_id=1, source_target_pairs={{0,16},{1,17},{2,18},{3,19},{4,20},{5,21},{6,22},{7,23},{8,24},{9,... | collective-permute-start | bytes 172040 | tf_op jit(solution)/shard_map/ppermute | solution.py:224
  10.1 14.9 %collective-permute-start.2 = (bf16[14,32,128]{2,1,0:T(8,128)(2,1)S(1)}, bf16[14,32,128]{2,1,0:T(8,128)(2,1)S(1)}, u32[]{:S(2)}, u32[]{:S(2)}) collective-permute-start(bf16[14,32,128]{2,1,0:T(8,128)(2,1)S(1)} %get-tuple-element.6.refs_0_), channel_id=1, source_target_pairs={{0,3},{1,2},{2,1},{3,0},{4,7},{5,6},{6,5},{7,4},{8,11},{9,10},{10,... | collective-permute-start | bytes 344072 | tf_op jit(solution)/shard_map/ppermute | solution.py:219
  11.2 7.6 %collective-permute-start.13 = (bf16[14,16,128]{2,1,0:T(8,128)(2,1)S(1)}, bf16[14,16,128]{2,1,0:T(8,128)(2,1)S(1)}, u32[]{:S(2)}, u32[]{:S(2)}) collective-permute-start(bf16[14,16,128]{2,1,0:T(8,128)(2,1)S(1)} %get-tuple-element.9), channel_id=1, source_target_pairs={{0,28},{1,29},{2,30},{3,31},{4,24},{5,25},{6,26},{7,27},{8,20},{9,... | collective-permute-start | bytes 172040 | tf_op jit(solution)/shard_map/ppermute | solution.py:224
  15.8 6.5 %collective-permute-start.12 = (bf16[14,16,128]{2,1,0:T(8,128)(2,1)S(1)}, bf16[14,16,128]{2,1,0:T(8,128)(2,1)S(1)}, u32[]{:S(2)}, u32[]{:S(2)}) collective-permute-start(bf16[14,16,128]{2,1,0:T(8,128)(2,1)S(1)} %get-tuple-element.9), channel_id=1, source_target_pairs={{0,24},{1,25},{2,26},{3,27},{4,28},{5,29},{6,30},{7,31},{8,16},{9,... | collective-permute-start | bytes 172040 | tf_op jit(solution)/shard_map/ppermute | solution.py:224
  15.8 6.5 %collective-permute-start.11 = (bf16[14,16,128]{2,1,0:T(8,128)(2,1)S(1)}, bf16[14,16,128]{2,1,0:T(8,128)(2,1)S(1)}, u32[]{:S(2)}, u32[]{:S(2)}) collective-permute-start(bf16[14,16,128]{2,1,0:T(8,128)(2,1)S(1)} %get-tuple-element.9), channel_id=1, source_target_pairs={{0,20},{1,21},{2,22},{3,23},{4,16},{5,17},{6,18},{7,19},{8,28},{9,... | collective-permute-start | bytes 172040 | tf_op jit(solution)/shard_map/ppermute | solution.py:224
  18.5 6.2 %collective-permute-start.10 = (bf16[14,16,128]{2,1,0:T(8,128)(2,1)S(1)}, bf16[14,16,128]{2,1,0:T(8,128)(2,1)S(1)}, u32[]{:S(2)}, u32[]{:S(2)}) collective-permute-start(bf16[14,16,128]{2,1,0:T(8,128)(2,1)S(1)} %get-tuple-element.9), channel_id=1, source_target_pairs={{0,16},{1,17},{2,18},{3,19},{4,20},{5,21},{6,22},{7,23},{8,24},{9,... | collective-permute-start | bytes 172040 | tf_op jit(solution)/shard_map/ppermute | solution.py:224
  18.8 7.9 %collective-permute-start.1 = (bf16[14,32,128]{2,1,0:T(8,128)(2,1)S(1)}, bf16[14,32,128]{2,1,0:T(8,128)(2,1)S(1)}, u32[]{:S(2)}, u32[]{:S(2)}) collective-permute-start(bf16[14,32,128]{2,1,0:T(8,128)(2,1)S(1)} %get-tuple-element.6.refs_0_), channel_id=1, source_target_pairs={{0,2},{1,3},{2,0},{3,1},{4,6},{5,7},{6,4},{7,5},{8,10},{9,11},{10,... | collective-permute-start | bytes 344072 | tf_op jit(solution)/shard_map/ppermute | solution.py:219
  22.3 4.5 %collective-permute-start = (bf16[14,32,128]{2,1,0:T(8,128)(2,1)S(1)}, bf16[14,32,128]{2,1,0:T(8,128)(2,1)S(1)}, u32[]{:S(2)}, u32[]{:S(2)}) collective-permute-start(bf16[14,32,128]{2,1,0:T(8,128)(2,1)S(1)} %get-tuple-element.6.refs_0_), channel_id=1, source_target_pairs={{0,1},{1,0},{2,3},{3,2},{4,5},{5,4},{6,7},{7,6},{8,9},{9,8},{10,11... | collective-permute-start | bytes 344072 | tf_op jit(solution)/shard_map/ppermute | solution.py:219
  22.3 7.9 %collective-permute-start.9 = (bf16[14,32,128]{2,1,0:T(8,128)(2,1)S(1)}, bf16[14,32,128]{2,1,0:T(8,128)(2,1)S(1)}, u32[]{:S(2)}, u32[]{:S(2)}) collective-permute-start(bf16[14,32,128]{2,1,0:T(8,128)(2,1)S(1)} %get-tuple-element.8.refs_8_), channel_id=1, source_target_pairs={{0,12},{1,13},{2,14},{3,15},{4,8},{5,9},{6,10},{7,11},{8,4},{9,5},... | collective-permute-start | bytes 344072 | tf_op jit(solution)/shard_map/ppermute | solution.py:219
  24.7 9.8 %collective-permute-start.8 = (bf16[14,32,128]{2,1,0:T(8,128)(2,1)S(1)}, bf16[14,32,128]{2,1,0:T(8,128)(2,1)S(1)}, u32[]{:S(2)}, u32[]{:S(2)}) collective-permute-start(bf16[14,32,128]{2,1,0:T(8,128)(2,1)S(1)} %get-tuple-element.8.refs_8_), channel_id=1, source_target_pairs={{0,8},{1,9},{2,10},{3,11},{4,12},{5,13},{6,14},{7,15},{8,0},{9,1},... | collective-permute-start | bytes 344072 | tf_op jit(solution)/shard_map/ppermute | solution.py:219
  25.0 9.6 %collective-permute-start.7 = (bf16[14,32,128]{2,1,0:T(8,128)(2,1)S(1)}, bf16[14,32,128]{2,1,0:T(8,128)(2,1)S(1)}, u32[]{:S(2)}, u32[]{:S(2)}) collective-permute-start(bf16[14,32,128]{2,1,0:T(8,128)(2,1)S(1)} %get-tuple-element.8.refs_8_), channel_id=1, source_target_pairs={{0,4},{1,5},{2,6},{3,7},{4,0},{5,1},{6,2},{7,3},{8,12},{9,13},{10,... | collective-permute-start | bytes 344072 | tf_op jit(solution)/shard_map/ppermute | solution.py:219
  40.2 3.0 %collective-permute-start.16 = (f32[8,128]{1,0:T(8,128)S(1)}, f32[8,128]{1,0:T(8,128)S(1)}, u32[]{:S(2)}, u32[]{:S(2)}) collective-permute-start(f32[8,128]{1,0:T(8,128)S(1)} %terms.1), channel_id=1, source_target_pairs={{0,3},{1,2},{2,1},{3,0},{4,7},{5,6},{6,5},{7,4},{8,11},{9,10},{10,... | collective-permute-start | bytes 12296 | tf_op jit(solution)/shard_map/ppermute | solution.py:219
  40.9 3.6 %collective-permute-start.15 = (f32[8,128]{1,0:T(8,128)S(1)}, f32[8,128]{1,0:T(8,128)S(1)}, u32[]{:S(2)}, u32[]{:S(2)}) collective-permute-start(f32[8,128]{1,0:T(8,128)S(1)} %terms.1), channel_id=1, source_target_pairs={{0,2},{1,3},{2,0},{3,1},{4,6},{5,7},{6,4},{7,5},{8,10},{9,11},{10,... | collective-permute-start | bytes 12296 | tf_op jit(solution)/shard_map/ppermute | solution.py:219
  41.8 2.7 %collective-permute-start.14 = (f32[8,128]{1,0:T(8,128)S(1)}, f32[8,128]{1,0:T(8,128)S(1)}, u32[]{:S(2)}, u32[]{:S(2)}) collective-permute-start(f32[8,128]{1,0:T(8,128)S(1)} %terms.1), channel_id=1, source_target_pairs={{0,1},{1,0},{2,3},{3,2},{4,5},{5,4},{6,7},{7,6},{8,9},{9,8},{10,11... | collective-permute-start | bytes 12296 | tf_op jit(solution)/shard_map/ppermute | solution.py:219
  44.5 9.1 %collective-permute-start.23 = (f32[8,128]{1,0:T(8,128)S(1)}, f32[8,128]{1,0:T(8,128)S(1)}, u32[]{:S(2)}, u32[]{:S(2)}) collective-permute-start(f32[8,128]{1,0:T(8,128)S(1)} %add_add_fusion.refs_0_), channel_id=1, source_target_pairs={{0,28},{1,29},{2,30},{3,31},{4,24},{5,25},{6,26},{7,27},{8,20},{9,... | collective-permute-start | bytes 12296 | tf_op jit(solution)/shard_map/ppermute | solution.py:224
  47.2 6.3 %collective-permute-start.22 = (f32[8,128]{1,0:T(8,128)S(1)}, f32[8,128]{1,0:T(8,128)S(1)}, u32[]{:S(2)}, u32[]{:S(2)}) collective-permute-start(f32[8,128]{1,0:T(8,128)S(1)} %add_add_fusion.refs_0_), channel_id=1, source_target_pairs={{0,24},{1,25},{2,26},{3,27},{4,28},{5,29},{6,30},{7,31},{8,16},{9,... | collective-permute-start | bytes 12296 | tf_op jit(solution)/shard_map/ppermute | solution.py:224
  47.2 8.5 %collective-permute-start.21 = (f32[8,128]{1,0:T(8,128)S(1)}, f32[8,128]{1,0:T(8,128)S(1)}, u32[]{:S(2)}, u32[]{:S(2)}) collective-permute-start(f32[8,128]{1,0:T(8,128)S(1)} %add_add_fusion.refs_0_), channel_id=1, source_target_pairs={{0,20},{1,21},{2,22},{3,23},{4,16},{5,17},{6,18},{7,19},{8,28},{9,... | collective-permute-start | bytes 12296 | tf_op jit(solution)/shard_map/ppermute | solution.py:224
  50.1 5.6 %collective-permute-start.20 = (f32[8,128]{1,0:T(8,128)S(1)}, f32[8,128]{1,0:T(8,128)S(1)}, u32[]{:S(2)}, u32[]{:S(2)}) collective-permute-start(f32[8,128]{1,0:T(8,128)S(1)} %add_add_fusion.refs_0_), channel_id=1, source_target_pairs={{0,16},{1,17},{2,18},{3,19},{4,20},{5,21},{6,22},{7,23},{8,24},{9,... | collective-permute-start | bytes 12296 | tf_op jit(solution)/shard_map/ppermute | solution.py:224
  51.3 5.4 %collective-permute-start.19 = (f32[8,128]{1,0:T(8,128)S(1)}, f32[8,128]{1,0:T(8,128)S(1)}, u32[]{:S(2)}, u32[]{:S(2)}) collective-permute-start(f32[8,128]{1,0:T(8,128)S(1)} %add_add_fusion.refs_0_), channel_id=1, source_target_pairs={{0,12},{1,13},{2,14},{3,15},{4,8},{5,9},{6,10},{7,11},{8,4},{9,5},... | collective-permute-start | bytes 12296 | tf_op jit(solution)/shard_map/ppermute | solution.py:219
  53.6 4.5 %collective-permute-start.18 = (f32[8,128]{1,0:T(8,128)S(1)}, f32[8,128]{1,0:T(8,128)S(1)}, u32[]{:S(2)}, u32[]{:S(2)}) collective-permute-start(f32[8,128]{1,0:T(8,128)S(1)} %add_add_fusion.refs_0_), channel_id=1, source_target_pairs={{0,8},{1,9},{2,10},{3,11},{4,12},{5,13},{6,14},{7,15},{8,0},{9,1},... | collective-permute-start | bytes 12296 | tf_op jit(solution)/shard_map/ppermute | solution.py:219
  53.6 4.5 %collective-permute-start.17 = (f32[8,128]{1,0:T(8,128)S(1)}, f32[8,128]{1,0:T(8,128)S(1)}, u32[]{:S(2)}, u32[]{:S(2)}) collective-permute-start(f32[8,128]{1,0:T(8,128)S(1)} %add_add_fusion.refs_0_), channel_id=1, source_target_pairs={{0,4},{1,5},{2,6},{3,7},{4,0},{5,1},{6,2},{7,3},{8,12},{9,13},{10,... | collective-permute-start | bytes 12296 | tf_op jit(solution)/shard_map/ppermute | solution.py:219
  (11 other events, 32.6 us)

commit v2 on v1

--- a/solution.py
+++ b/solution.py
@@ -177,15 +177,19 @@
     )
 
 
-def final_kernel(*refs):
-    own, other = refs[0:4], refs[4:8]
-    ridge_ref, gram_ref, factor_ref = refs[8:]
-    panel = rows_of((own[0][...] + own[1][...]) + (own[2][...] + own[3][...]), 4)
-    cross = rows_of((other[0][...] + other[1][...]) + (other[2][...] + other[3][...]), 2)
+def tree_sum(values):
+    while len(values) > 1:
+        values = [a + b for a, b in zip(values[0::2], values[1::2])]
+    return values[0]
+
+
+def final_kernel(terms_ref, ridge_ref, gram_ref, factor_ref):
+    count = terms_ref.shape[0] // 2
+    sums = [tree_sum([terms_ref[g * count + i] for i in range(count)]) for g in range(2)]
+    first = lax.axis_index("rows") == 0
+    panel = rows_of(jnp.where(first, sums[0], sums[1]), 4)
     gram_ref[...] = panel
-    first = lax.axis_index("rows") == 0
-    mine = panel[:PIV_DEV]
-    diag = jnp.concatenate([jnp.where(first, mine, cross), jnp.where(first, cross, mine)], axis=0)
+    diag = jnp.concatenate([rows_of(total, 2) for total in sums], axis=0)
     row_id = lax.broadcasted_iota(jnp.int32, (EX, EX), 0)
     col_id = lax.broadcasted_iota(jnp.int32, (EX, EX), 1)
     ridge = jnp.where(row_id == col_id, jnp.broadcast_to(ridge_ref[...], (EX, EX)), 0.0)
@@ -203,16 +207,16 @@
     factor_ref[...] = factor
 
 
-def final(own, other, ridge):
+def final(terms, ridge):
     vmem = pl.BlockSpec(memory_space=pltpu.VMEM)
     out = jax.ShapeDtypeStruct((EX, EX), F32)
     return pl.pallas_call(
         final_kernel,
         out_shape=(out, out),
-        in_specs=[vmem] * 9,
+        in_specs=[vmem] * 2,
         out_specs=(vmem, vmem),
         name="solve",
-    )(*own, *other, ridge.reshape(1, EX))
+    )(terms, ridge.reshape(1, EX))
 
 
 def exchange(value, count, flip):
@@ -233,11 +237,8 @@
     own_x = [xo] + [exchange(xo, count, f) for f in near]
     other_x = [exchange_across(xp, count, f) for f in (0,) + near]
     term = main(own_x + other_x + own_g + other_g)
-    terms = [term] + [exchange(term, count, f) for f in near]
-    part = (terms[0] + terms[1]) + (terms[2] + terms[3])
-    own = [part] + [exchange(part, count, f) for f in far]
-    other = [exchange_across(part, count, f) for f in (0,) + far]
-    return final(own, other, ridge)
+    terms = lax.all_to_all(jnp.broadcast_to(term, (2 * count, 8, LANES)), ("rows", "chan"), 0, 0)
+    return final(terms, ridge)
 
 
 def jacobian_block(grad_rows, input_rows):

time: 63 us -> 57.2 us (0.908)
  starting transfers between devices: 33.4 us -> 20.3 us
  blocking collectives: 0 us -> 12.5 us
  waiting for transfers between devices: 14.7 us -> 9.85 us
    all_to_all x0 -> x1, blocking collectives: none -> 12.5 us  [local_packed(): lax.all_to_all(jnp.broadcast_to(term, (2 * count, 8, LANES)), ('rows', 'c...]
    ppermute x12 -> x8, starting transfers between devices: 20.1 us -> 13.3 us  [exchange_across(): return lax.ppermute(value, ('rows', 'chan'), pairs)]
    ppermute x12 -> x6, starting transfers between devices: 13.3 us -> 7.03 us  [exchange(): return lax.ppermute(value, 'chan', [(i, i ^ flip) for i in range(count)])]
    ppermute x12 -> x6, waiting for transfers between devices: 12.6 us -> 7.82 us  [exchange(): return lax.ppermute(value, 'chan', [(i, i ^ flip) for i in range(count)])]
    unnamed x22 -> x6, local copies, waits for them, and re-layouts: 3.16 us -> 2.6 us
    ppermute x12 -> x8, waiting for transfers between devices: 2.04 us -> 2.03 us  [exchange_across(): return lax.ppermute(value, ('rows', 'chan'), pairs)]
  transfers between devices with their start and end apart: 24 -> 14, of which waited for: 8 -> 4; matrix products, arithmetic and copies ran while one was open for 0% -> 0% of each run, Pallas kernels for 0% -> 0%
where the time goes in v2:
time: 57.2 us; the launch traced here: 56.9 us
  starting transfers between devices  20.3 us (35%)
  blocking collectives  12.5 us (22%)
  Pallas kernels  11 us (19%)
  waiting for transfers between devices  9.85 us (17%)
  local copies, waits for them, and re-layouts  2.61 us (5%)
  between operations  0.66 us (1%)
    ppermute x8, starting transfers between devices, exchange_across(): return lax.ppermute(value, ('rows', 'chan'), pairs)  13.3 us
    all_to_all x1, blocking collectives, local_packed(): lax.all_to_all(jnp.broadcast_to(term, (2 * count, 8, LANES)), ('rows', 'c...  12.5 us
    ppermute x6, waiting for transfers between devices, exchange(): return lax.ppermute(value, 'chan', [(i, i ^ flip) for i in range(count)])  7.82 us
    ppermute x6, starting transfers between devices, exchange(): return lax.ppermute(value, 'chan', [(i, i ^ flip) for i in range(count)])  7.03 us
    pallas_call x1, Pallas kernels, main(): pl.pallas_call(main_kernel, out_shape=jax.ShapeDtypeStruct((8, LANES), F3...  5.59 us
    pallas_call x1, Pallas kernels, final(): pl.pallas_call(final_kernel, out_shape=(out, out), in_specs=[vmem] * 2, o...  4.3 us
    unnamed x6, local copies, waits for them, and re-layouts  2.6 us
    ppermute x8, waiting for transfers between devices, exchange_across(): return lax.ppermute(value, ('rows', 'chan'), pairs)  2.03 us
  transfers between devices with their start and end apart: 14, of which 4 were waited for; matrix products, arithmetic and copies ran while one was open for 0% of the time, Pallas kernels for 0%

profile of v2, /device:TPU:0, one launch (start us, length us, event | category | flops | bytes accessed | tf_op | source)
XLA Modules:
  0.0 56.9 jit_solution(2559205485920699175)
XLA Ops:
  0.6 0.6 %copy-done.2 = s32[1,32]{1,0:T(1,128)S(1)} copy-done((s32[1,32]{1,0:T(1,128)S(1)}, s32[1,32]{1,0:T(1,128)}, u32[]{:S(2)}) %copy-start.2) | copy-done | bytes 152
  1.3 1.0 %copy-done = bf16[32,7,7,32]{3,0,2,1:T(8,128)(2,1)S(1)} copy-done((bf16[32,7,7,32]{3,0,2,1:T(8,128)(2,1)S(1)}, bf16[32,7,7,32]{3,0,2,1:T(8,128)(2,1)}, u32[]{:S(2)}) %copy-start) | copy-done | bytes 100376
  2.3 0.9 %copy-done.1 = bf16[32,32,49]{2,1,0:T(8,128)(2,1)S(1)} copy-done((bf16[32,32,49]{2,1,0:T(8,128)(2,1)S(1)}, bf16[32,32,49]{2,1,0:T(8,128)(2,1)}, u32[]{:S(2)}) %copy-start.1) | copy-done | bytes 100376
  3.2 1.1 %prep.1 = (bf16[14,32,128]{2,1,0:T(8,128)(2,1)S(1)}, bf16[14,32,128]{2,1,0:T(8,128)(2,1)S(1)}, bf16[14,16,128]{2,1,0:T(8,128)(2,1)S(1)}, bf16[14,16,128]{2,1,0:T(8,128)(2,1)S(1)}) custom-call(s32[1,32]{1,0:T(1,128)S(1)} %copy-done.2, bf16[49,32,32]{2,1,0:T(8,128)(2,1)S(1)} %bitcast.4, bf16[32,32,49]{2,1,0:T(8,128)(2,1)S(1)} %copy-done.1), custom_call_target="tpu_custom_call" | custom-call | tf_op jit(solution)/shard_map/prep/pallas_call | solution.py:65
  4.4 3.4 %collective-permute-start.6 = (bf16[14,16,128]{2,1,0:T(8,128)(2,1)S(1)}, bf16[14,16,128]{2,1,0:T(8,128)(2,1)S(1)}, u32[]{:S(2)}, u32[]{:S(2)}) collective-permute-start(bf16[14,16,128]{2,1,0:T(8,128)(2,1)S(1)} %get-tuple-element.7), channel_id=1, source_target_pairs={{0,19},{1,18},{2,17},{3,16},{4,23},{5,22},{6,21},{7,20},{8,27},{9,... | collective-permute-start | bytes 172040 | tf_op jit(solution)/shard_map/ppermute | solution.py:228
  7.8 0.6 %collective-permute-start.5 = (bf16[14,16,128]{2,1,0:T(8,128)(2,1)S(1)}, bf16[14,16,128]{2,1,0:T(8,128)(2,1)S(1)}, u32[]{:S(2)}, u32[]{:S(2)}) collective-permute-start(bf16[14,16,128]{2,1,0:T(8,128)(2,1)S(1)} %get-tuple-element.7), channel_id=1, source_target_pairs={{0,18},{1,19},{2,16},{3,17},{4,22},{5,23},{6,20},{7,21},{8,26},{9,... | collective-permute-start | bytes 172040 | tf_op jit(solution)/shard_map/ppermute | solution.py:228
  8.4 1.4 %collective-permute-start.4 = (bf16[14,16,128]{2,1,0:T(8,128)(2,1)S(1)}, bf16[14,16,128]{2,1,0:T(8,128)(2,1)S(1)}, u32[]{:S(2)}, u32[]{:S(2)}) collective-permute-start(bf16[14,16,128]{2,1,0:T(8,128)(2,1)S(1)} %get-tuple-element.7), channel_id=1, source_target_pairs={{0,17},{1,16},{2,19},{3,18},{4,21},{5,20},{6,23},{7,22},{8,25},{9,... | collective-permute-start | bytes 172040 | tf_op jit(solution)/shard_map/ppermute | solution.py:228
  9.8 0.3 collective-permute-start.3
  10.1 1.2 %collective-permute-start.2 = (bf16[14,32,128]{2,1,0:T(8,128)(2,1)S(1)}, bf16[14,32,128]{2,1,0:T(8,128)(2,1)S(1)}, u32[]{:S(2)}, u32[]{:S(2)}) collective-permute-start(bf16[14,32,128]{2,1,0:T(8,128)(2,1)S(1)} %get-tuple-element.6.refs_0_), channel_id=1, source_target_pairs={{0,3},{1,2},{2,1},{3,0},{4,7},{5,6},{6,5},{7,4},{8,11},{9,10},{10,... | collective-permute-start | bytes 344072 | tf_op jit(solution)/shard_map/ppermute | solution.py:223
  11.2 4.5 %collective-permute-start.13 = (bf16[14,16,128]{2,1,0:T(8,128)(2,1)S(1)}, bf16[14,16,128]{2,1,0:T(8,128)(2,1)S(1)}, u32[]{:S(2)}, u32[]{:S(2)}) collective-permute-start(bf16[14,16,128]{2,1,0:T(8,128)(2,1)S(1)} %get-tuple-element.9), channel_id=1, source_target_pairs={{0,28},{1,29},{2,30},{3,31},{4,24},{5,25},{6,26},{7,27},{8,20},{9,... | collective-permute-start | bytes 172040 | tf_op jit(solution)/shard_map/ppermute | solution.py:228
  15.8 0.0 collective-permute-start.12
  15.8 2.7 %collective-permute-start.11 = (bf16[14,16,128]{2,1,0:T(8,128)(2,1)S(1)}, bf16[14,16,128]{2,1,0:T(8,128)(2,1)S(1)}, u32[]{:S(2)}, u32[]{:S(2)}) collective-permute-start(bf16[14,16,128]{2,1,0:T(8,128)(2,1)S(1)} %get-tuple-element.9), channel_id=1, source_target_pairs={{0,20},{1,21},{2,22},{3,23},{4,16},{5,17},{6,18},{7,19},{8,28},{9,... | collective-permute-start | bytes 172040 | tf_op jit(solution)/shard_map/ppermute | solution.py:228
  18.5 0.3 collective-permute-start.10
  18.8 1.5 %collective-permute-start.1 = (bf16[14,32,128]{2,1,0:T(8,128)(2,1)S(1)}, bf16[14,32,128]{2,1,0:T(8,128)(2,1)S(1)}, u32[]{:S(2)}, u32[]{:S(2)}) collective-permute-start(bf16[14,32,128]{2,1,0:T(8,128)(2,1)S(1)} %get-tuple-element.6.refs_0_), channel_id=1, source_target_pairs={{0,2},{1,3},{2,0},{3,1},{4,6},{5,7},{6,4},{7,5},{8,10},{9,11},{10,... | collective-permute-start | bytes 344072 | tf_op jit(solution)/shard_map/ppermute | solution.py:223
  20.3 1.9 %collective-permute-done.12.refs_14_ = bf16[14,16,128]{2,1,0:T(8,128)(2,1)S(1)} collective-permute-done((bf16[14,16,128]{2,1,0:T(8,128)(2,1)S(1)}, bf16[14,16,128]{2,1,0:T(8,128)(2,1)S(1)}, u32[]{:S(2)}, u32[]{:S(2)}) %collective-permute-start.12) | collective-permute-done | bytes 57376 | tf_op jit(solution)/shard_map/ppermute | solution.py:228
  22.3 0.1 collective-permute-done.11.refs_13_
  22.3 2.4 %collective-permute-start.9 = (bf16[14,32,128]{2,1,0:T(8,128)(2,1)S(1)}, bf16[14,32,128]{2,1,0:T(8,128)(2,1)S(1)}, u32[]{:S(2)}, u32[]{:S(2)}) collective-permute-start(bf16[14,32,128]{2,1,0:T(8,128)(2,1)S(1)} %get-tuple-element.8.refs_8_), channel_id=1, source_target_pairs={{0,12},{1,13},{2,14},{3,15},{4,8},{5,9},{6,10},{7,11},{8,4},{9,5},... | collective-permute-start | bytes 344072 | tf_op jit(solution)/shard_map/ppermute | solution.py:223
  24.7 0.2 collective-permute-start.8
  25.0 1.8 %collective-permute-start.7 = (bf16[14,32,128]{2,1,0:T(8,128)(2,1)S(1)}, bf16[14,32,128]{2,1,0:T(8,128)(2,1)S(1)}, u32[]{:S(2)}, u32[]{:S(2)}) collective-permute-start(bf16[14,32,128]{2,1,0:T(8,128)(2,1)S(1)} %get-tuple-element.8.refs_8_), channel_id=1, source_target_pairs={{0,4},{1,5},{2,6},{3,7},{4,0},{5,1},{6,2},{7,3},{8,12},{9,13},{10,... | collective-permute-start | bytes 344072 | tf_op jit(solution)/shard_map/ppermute | solution.py:223
  26.7 3.5 %collective-permute-done.9.refs_11_ = bf16[14,32,128]{2,1,0:T(8,128)(2,1)S(1)} collective-permute-done((bf16[14,32,128]{2,1,0:T(8,128)(2,1)S(1)}, bf16[14,32,128]{2,1,0:T(8,128)(2,1)S(1)}, u32[]{:S(2)}, u32[]{:S(2)}) %collective-permute-start.9) | collective-permute-done | bytes 114720 | tf_op jit(solution)/shard_map/ppermute | solution.py:223
  30.2 4.3 %collective-permute-done.8.refs_10_ = bf16[14,32,128]{2,1,0:T(8,128)(2,1)S(1)} collective-permute-done((bf16[14,32,128]{2,1,0:T(8,128)(2,1)S(1)}, bf16[14,32,128]{2,1,0:T(8,128)(2,1)S(1)}, u32[]{:S(2)}, u32[]{:S(2)}) %collective-permute-start.8) | collective-permute-done | bytes 114720 | tf_op jit(solution)/shard_map/ppermute | solution.py:223
  34.6 5.6 %terms.1 = f32[8,128]{1,0:T(8,128)S(1)} custom-call(bf16[14,32,128]{2,1,0:T(8,128)(2,1)S(1)} %get-tuple-element.6.refs_0_, bf16[14,32,128]{2,1,0:T(8,128)(2,1)S(1)} %collective-permute-done.refs_1_, bf16[14,32,128]{2,1,0:T(8,128)(2,1)S(1)} %collective-permute-done.1.refs_2_, bf16[14,32,128]{2,1,0:T(8,128)(2,1)S(1)} %collective-permute-done.2.refs_3_, ...), custom_call_target="tpu_custom_call" | custom-call | tf_op jit(solution)/shard_map/terms/pallas_call | solution.py:157
  40.2 12.5 %all_to_all.5.terms_ref = f32[32,8,128]{2,1,0:T(8,128)} all-to-all(f32[32,8,128]{2,1,0:T(8,128)S(1)} %broadcast_in_dim.3), channel_id=1, replica_groups=mesh['rows'=2,'chan'=16] {'rows','chan'}, dimensions={0} | all-to-all | bytes 262144 | tf_op jit(solution)/shard_map/all_to_all | solution.py:240
  52.6 4.3 %solve.1 = (f32[32,32]{1,0:T(8,128)}, f32[32,32]{1,0:T(8,128)}) custom-call(f32[32,8,128]{2,1,0:T(8,128)} %all_to_all.5.terms_ref, f32[1,32]{1,0:T(1,128)} %bitcast.5), custom_call_target="tpu_custom_call" | custom-call | tf_op jit(solution)/shard_map/solve/pallas_call | solution.py:213
  (15 shorter events, 0.0 us)
Async XLA Ops:
  0.6 0.7 %copy-start.2 = (s32[1,32]{1,0:T(1,128)S(1)}, s32[1,32]{1,0:T(1,128)}, u32[]{:S(2)}) copy-start(s32[1,32]{1,0:T(1,128)} %order_ref.1) | copy-start | bytes 388
  1.3 1.0 %copy-start = (bf16[32,7,7,32]{3,0,2,1:T(8,128)(2,1)S(1)}, bf16[32,7,7,32]{3,0,2,1:T(8,128)(2,1)}, u32[]{:S(2)}) copy-start(bf16[32,7,7,32]{3,0,2,1:T(8,128)(2,1)} %param.4) | copy-start | bytes 301060
  2.3 0.9 %copy-start.1 = (bf16[32,32,49]{2,1,0:T(8,128)(2,1)S(1)}, bf16[32,32,49]{2,1,0:T(8,128)(2,1)}, u32[]{:S(2)}) copy-start(bf16[32,32,49]{2,1,0:T(8,128)(2,1)} %g_ref.1) | copy-start | bytes 301060
  4.4 6.9 %collective-permute-start.6 = (bf16[14,16,128]{2,1,0:T(8,128)(2,1)S(1)}, bf16[14,16,128]{2,1,0:T(8,128)(2,1)S(1)}, u32[]{:S(2)}, u32[]{:S(2)}) collective-permute-start(bf16[14,16,128]{2,1,0:T(8,128)(2,1)S(1)} %get-tuple-element.7), channel_id=1, source_target_pairs={{0,19},{1,18},{2,17},{3,16},{4,23},{5,22},{6,21},{7,20},{8,27},{9,... | collective-permute-start | bytes 172040 | tf_op jit(solution)/shard_map/ppermute | solution.py:228
  7.8 8.0 %collective-permute-start.5 = (bf16[14,16,128]{2,1,0:T(8,128)(2,1)S(1)}, bf16[14,16,128]{2,1,0:T(8,128)(2,1)S(1)}, u32[]{:S(2)}, u32[]{:S(2)}) collective-permute-start(bf16[14,16,128]{2,1,0:T(8,128)(2,1)S(1)} %get-tuple-element.7), channel_id=1, source_target_pairs={{0,18},{1,19},{2,16},{3,17},{4,22},{5,23},{6,20},{7,21},{8,26},{9,... | collective-permute-start | bytes 172040 | tf_op jit(solution)/shard_map/ppermute | solution.py:228
  8.4 7.4 %collective-permute-start.4 = (bf16[14,16,128]{2,1,0:T(8,128)(2,1)S(1)}, bf16[14,16,128]{2,1,0:T(8,128)(2,1)S(1)}, u32[]{:S(2)}, u32[]{:S(2)}) collective-permute-start(bf16[14,16,128]{2,1,0:T(8,128)(2,1)S(1)} %get-tuple-element.7), channel_id=1, source_target_pairs={{0,17},{1,16},{2,19},{3,18},{4,21},{5,20},{6,23},{7,22},{8,25},{9,... | collective-permute-start | bytes 172040 | tf_op jit(solution)/shard_map/ppermute | solution.py:228
  9.8 8.8 %collective-permute-start.3 = (bf16[14,16,128]{2,1,0:T(8,128)(2,1)S(1)}, bf16[14,16,128]{2,1,0:T(8,128)(2,1)S(1)}, u32[]{:S(2)}, u32[]{:S(2)}) collective-permute-start(bf16[14,16,128]{2,1,0:T(8,128)(2,1)S(1)} %get-tuple-element.7), channel_id=1, source_target_pairs={{0,16},{1,17},{2,18},{3,19},{4,20},{5,21},{6,22},{7,23},{8,24},{9,... | collective-permute-start | bytes 172040 | tf_op jit(solution)/shard_map/ppermute | solution.py:228
  10.1 14.9 %collective-permute-start.2 = (bf16[14,32,128]{2,1,0:T(8,128)(2,1)S(1)}, bf16[14,32,128]{2,1,0:T(8,128)(2,1)S(1)}, u32[]{:S(2)}, u32[]{:S(2)}) collective-permute-start(bf16[14,32,128]{2,1,0:T(8,128)(2,1)S(1)} %get-tuple-element.6.refs_0_), channel_id=1, source_target_pairs={{0,3},{1,2},{2,1},{3,0},{4,7},{5,6},{6,5},{7,4},{8,11},{9,10},{10,... | collective-permute-start | bytes 344072 | tf_op jit(solution)/shard_map/ppermute | solution.py:223
  11.2 7.6 %collective-permute-start.13 = (bf16[14,16,128]{2,1,0:T(8,128)(2,1)S(1)}, bf16[14,16,128]{2,1,0:T(8,128)(2,1)S(1)}, u32[]{:S(2)}, u32[]{:S(2)}) collective-permute-start(bf16[14,16,128]{2,1,0:T(8,128)(2,1)S(1)} %get-tuple-element.9), channel_id=1, source_target_pairs={{0,28},{1,29},{2,30},{3,31},{4,24},{5,25},{6,26},{7,27},{8,20},{9,... | collective-permute-start | bytes 172040 | tf_op jit(solution)/shard_map/ppermute | solution.py:228
  15.8 6.5 %collective-permute-start.12 = (bf16[14,16,128]{2,1,0:T(8,128)(2,1)S(1)}, bf16[14,16,128]{2,1,0:T(8,128)(2,1)S(1)}, u32[]{:S(2)}, u32[]{:S(2)}) collective-permute-start(bf16[14,16,128]{2,1,0:T(8,128)(2,1)S(1)} %get-tuple-element.9), channel_id=1, source_target_pairs={{0,24},{1,25},{2,26},{3,27},{4,28},{5,29},{6,30},{7,31},{8,16},{9,... | collective-permute-start | bytes 172040 | tf_op jit(solution)/shard_map/ppermute | solution.py:228
  15.8 6.6 %collective-permute-start.11 = (bf16[14,16,128]{2,1,0:T(8,128)(2,1)S(1)}, bf16[14,16,128]{2,1,0:T(8,128)(2,1)S(1)}, u32[]{:S(2)}, u32[]{:S(2)}) collective-permute-start(bf16[14,16,128]{2,1,0:T(8,128)(2,1)S(1)} %get-tuple-element.9), channel_id=1, source_target_pairs={{0,20},{1,21},{2,22},{3,23},{4,16},{5,17},{6,18},{7,19},{8,28},{9,... | collective-permute-start | bytes 172040 | tf_op jit(solution)/shard_map/ppermute | solution.py:228
  18.5 6.2 %collective-permute-start.10 = (bf16[14,16,128]{2,1,0:T(8,128)(2,1)S(1)}, bf16[14,16,128]{2,1,0:T(8,128)(2,1)S(1)}, u32[]{:S(2)}, u32[]{:S(2)}) collective-permute-start(bf16[14,16,128]{2,1,0:T(8,128)(2,1)S(1)} %get-tuple-element.9), channel_id=1, source_target_pairs={{0,16},{1,17},{2,18},{3,19},{4,20},{5,21},{6,22},{7,23},{8,24},{9,... | collective-permute-start | bytes 172040 | tf_op jit(solution)/shard_map/ppermute | solution.py:228
  18.8 7.9 %collective-permute-start.1 = (bf16[14,32,128]{2,1,0:T(8,128)(2,1)S(1)}, bf16[14,32,128]{2,1,0:T(8,128)(2,1)S(1)}, u32[]{:S(2)}, u32[]{:S(2)}) collective-permute-start(bf16[14,32,128]{2,1,0:T(8,128)(2,1)S(1)} %get-tuple-element.6.refs_0_), channel_id=1, source_target_pairs={{0,2},{1,3},{2,0},{3,1},{4,6},{5,7},{6,4},{7,5},{8,10},{9,11},{10,... | collective-permute-start | bytes 344072 | tf_op jit(solution)/shard_map/ppermute | solution.py:223
  22.3 4.5 %collective-permute-start = (bf16[14,32,128]{2,1,0:T(8,128)(2,1)S(1)}, bf16[14,32,128]{2,1,0:T(8,128)(2,1)S(1)}, u32[]{:S(2)}, u32[]{:S(2)}) collective-permute-start(bf16[14,32,128]{2,1,0:T(8,128)(2,1)S(1)} %get-tuple-element.6.refs_0_), channel_id=1, source_target_pairs={{0,1},{1,0},{2,3},{3,2},{4,5},{5,4},{6,7},{7,6},{8,9},{9,8},{10,11... | collective-permute-start | bytes 344072 | tf_op jit(solution)/shard_map/ppermute | solution.py:223
  22.3 7.9 %collective-permute-start.9 = (bf16[14,32,128]{2,1,0:T(8,128)(2,1)S(1)}, bf16[14,32,128]{2,1,0:T(8,128)(2,1)S(1)}, u32[]{:S(2)}, u32[]{:S(2)}) collective-permute-start(bf16[14,32,128]{2,1,0:T(8,128)(2,1)S(1)} %get-tuple-element.8.refs_8_), channel_id=1, source_target_pairs={{0,12},{1,13},{2,14},{3,15},{4,8},{5,9},{6,10},{7,11},{8,4},{9,5},... | collective-permute-start | bytes 344072 | tf_op jit(solution)/shard_map/ppermute | solution.py:223
  24.7 9.8 %collective-permute-start.8 = (bf16[14,32,128]{2,1,0:T(8,128)(2,1)S(1)}, bf16[14,32,128]{2,1,0:T(8,128)(2,1)S(1)}, u32[]{:S(2)}, u32[]{:S(2)}) collective-permute-start(bf16[14,32,128]{2,1,0:T(8,128)(2,1)S(1)} %get-tuple-element.8.refs_8_), channel_id=1, source_target_pairs={{0,8},{1,9},{2,10},{3,11},{4,12},{5,13},{6,14},{7,15},{8,0},{9,1},... | collective-permute-start | bytes 344072 | tf_op jit(solution)/shard_map/ppermute | solution.py:223
  25.0 9.6 %collective-permute-start.7 = (bf16[14,32,128]{2,1,0:T(8,128)(2,1)S(1)}, bf16[14,32,128]{2,1,0:T(8,128)(2,1)S(1)}, u32[]{:S(2)}, u32[]{:S(2)}) collective-permute-start(bf16[14,32,128]{2,1,0:T(8,128)(2,1)S(1)} %get-tuple-element.8.refs_8_), channel_id=1, source_target_pairs={{0,4},{1,5},{2,6},{3,7},{4,0},{5,1},{6,2},{7,3},{8,12},{9,13},{10,... | collective-permute-start | bytes 344072 | tf_op jit(solution)/shard_map/ppermute | solution.py:223

commit v3 on v2

--- a/solution.py
+++ b/solution.py
@@ -19,7 +19,7 @@
 BF16 = jnp.bfloat16
 
 
-def prep_kernel(order_ref, x_ref, g_ref, xo_ref, go_ref, xp_ref, gp_ref, gs, gt, gout):
+def prep_kernel(order_ref, x_ref, g_ref, xo_ref, go_ref, gs, gt, gout):
     row_id = lax.broadcasted_iota(jnp.int32, (EX, EX), 0)
     col_id = lax.broadcasted_iota(jnp.int32, (EX, EX), 1)
     onehot = jnp.zeros((EX, EX), F32)
@@ -35,9 +35,7 @@
             py, px = group // 2, (group % 2) * 4 + j
             pieces.append(x_ref[py * SIDE + px] if px < SIDE else zero_block)
         packed = jnp.concatenate(pieces, axis=1)
-        ordered = jnp.dot(onehot, packed, preferred_element_type=F32).astype(BF16)
-        xo_ref[group] = ordered
-        xp_ref[group] = ordered[:PIV_DEV]
+        xo_ref[group] = jnp.dot(onehot, packed, preferred_element_type=F32).astype(BF16)
     block_id = lax.broadcasted_iota(jnp.int32, (GROUPS4, LANES), 1) // CH
     for quad in range(EX // 4):
         flipped = jnp.transpose(gs[quad * LANES:(quad + 1) * LANES, :])
@@ -53,20 +51,17 @@
                 merged = jnp.where(block_id == j, moved, merged)
             gout[pl.ds(quad * 4 + e, GROUPS4, stride=EX), :] = merged
     for group in range(GROUPS4):
-        ordered = gout[group * EX:(group + 1) * EX, :].astype(BF16)
-        go_ref[group] = ordered
-        gp_ref[group] = ordered[:PIV_DEV]
+        go_ref[group] = gout[group * EX:(group + 1) * EX, :].astype(BF16)
 
 
 def prep(order, x, g):
     full = jax.ShapeDtypeStruct((GROUPS4, EX, LANES), BF16)
-    part = jax.ShapeDtypeStruct((GROUPS4, PIV_DEV, LANES), BF16)
     vmem = pl.BlockSpec(memory_space=pltpu.VMEM)
     return pl.pallas_call(
         prep_kernel,
-        out_shape=(full, full, part, part),
+        out_shape=(full, full),
         in_specs=[pl.BlockSpec(memory_space=pltpu.SMEM), vmem, vmem],
-        out_specs=(vmem,) * 4,
+        out_specs=(vmem,) * 2,
         scratch_shapes=[
             pltpu.VMEM((EX * CH, LANES), F32),
             pltpu.VMEM((SIDE * PITCH, LANES), F32),
@@ -77,97 +72,116 @@
     )(order, x, g)
 
 
-def unpack(refs, group):
-    values = [ref[group] for ref in refs]
-    return [
-        jnp.concatenate([v[:, j * CH:(j + 1) * CH] for v in values], axis=1)
-        for j in range(4)
-    ]
-
-
+SPOTS = SIDE * SIDE
 ROWB = SIDE * EX
-COLB = PITCH * EX
-
-
-def main_kernel(*refs):
-    xo, xc, go, gc = refs[0:4], refs[4:8], refs[8:12], refs[12:16]
-    out_ref, lx, rx, lg, rg, t = refs[16:]
-    zero_rows = jnp.zeros((EX, LANES), BF16)
-    for py in range(SIDE):
-        first, last = py * ROWB, py * ROWB + ROWB - EX
-        lx[first:first + EX, 0:LANES] = zero_rows
-        lx[last:last + EX, 2 * LANES:3 * LANES] = zero_rows
-        first, last = py * COLB, py * COLB + COLB - EX
-        rx[first:first + EX, 0:LANES] = zero_rows
-        rx[last - EX:last, 2 * LANES:3 * LANES] = zero_rows
-        for d in range(3):
-            rx[last:last + EX, d * LANES:(d + 1) * LANES] = zero_rows
-        rg[last:last + EX, :] = zero_rows
+COLB = PITCH * PIV_DEV
+
+
+def cost(flops, moved):
+    return pl.CostEstimate(flops=flops, bytes_accessed=moved, transcendentals=0)
+
+
+def unpack_kernel(*refs):
+    sources, all_ref, piv_ref = refs[:4], refs[4], refs[5]
     for group in range(GROUPS4):
-        own_x, other_x = unpack(xo, group), unpack(xc, group)
-        own_g, other_g = unpack(go, group), unpack(gc, group)
+        values = [ref[group] for ref in sources]
         for j in range(4):
             py, px = group // 2, (group % 2) * 4 + j
             if px == SIDE:
                 continue
-            row, col = (py * SIDE + px) * EX, (py * PITCH + px) * EX
-            piv_x = jnp.concatenate([own_x[j][:PIV_DEV], other_x[j]], axis=0)
-            for d in (-1, 0, 1):
-                if 0 <= px - d < SIDE:
-                    lanes = slice((d + 1) * LANES, (d + 2) * LANES)
-                    lx[row - d * EX:row - d * EX + EX, lanes] = own_x[j]
-                    rx[col - d * EX:col - d * EX + EX, lanes] = piv_x
-            lg[row:row + EX, :] = own_g[j]
-            rg[col:col + EX, :] = jnp.concatenate([own_g[j][:PIV_DEV], other_g[j]], axis=0)
+            spot = jnp.concatenate([v[:, j * CH:(j + 1) * CH] for v in values], axis=1)
+            all_ref[py * SIDE + px] = spot
+            piv_ref[py * SIDE + px] = spot[:PIV_DEV]
+
+
+def unpack(arrays, name):
+    vmem = pl.BlockSpec(memory_space=pltpu.VMEM)
+    return pl.pallas_call(
+        unpack_kernel,
+        out_shape=(
+            jax.ShapeDtypeStruct((SPOTS, EX, LANES), BF16),
+            jax.ShapeDtypeStruct((SPOTS, PIV_DEV, LANES), BF16),
+        ),
+        in_specs=[vmem] * 4,
+        out_specs=(vmem,) * 2,
+        cost_estimate=cost(0, 1 << 20),
+        name=name,
+    )(*arrays)
+
+
+def panel_terms(x, g, xp, gp, lx, rx, rg, t):
+    for py in range(SIDE):
+        for px in range(PITCH):
+            row, col = (py * SIDE + px) * EX, (py * PITCH + px) * PIV_DEV
+            for d in range(3):
+                from_x = px + d - 1
+                inside = 0 <= from_x < SIDE and px < SIDE
+                lanes = slice(d * LANES, (d + 1) * LANES)
+                spot = py * SIDE + from_x
+                rx[col:col + PIV_DEV, lanes] = xp[spot] if inside else jnp.zeros((PIV_DEV, LANES), BF16)
+                if px < SIDE:
+                    lx[row:row + EX, lanes] = x[spot] if inside else jnp.zeros((EX, LANES), BF16)
+            rg[col:col + PIV_DEV, :] = gp[py * SIDE + px] if px < SIDE else jnp.zeros((PIV_DEV, LANES), BF16)
 
     contract = (((1,), (1,)), ((), ()))
-    for qy in range(SIDE):
-        right = rx[qy * COLB:(qy + 1) * COLB, :]
+    spans = [(qy, min(qy + 2, SIDE)) for qy in range(0, SIDE, 2)]
+    for start, stop in spans:
+        right = rx[start * COLB:stop * COLB, :]
         for py in range(SIDE):
             left = lx[py * ROWB:(py + 1) * ROWB, :]
-            t[py * SIDE + qy] = lax.dot_general(left, right, contract, preferred_element_type=F32)
+            t[py, :, start * COLB:stop * COLB] = lax.dot_general(left, right, contract, preferred_element_type=F32)
     acc = jnp.zeros((EX, COLB), F32)
-    for qy in range(SIDE):
-        right = rg[qy * COLB:(qy + 1) * COLB, :]
+    for start, stop in spans:
+        right = rg[start * COLB:stop * COLB, :]
         for py in range(SIDE):
-            left = lg[py * ROWB:(py + 1) * ROWB, :]
+            left = g[py * SIDE:(py + 1) * SIDE].reshape(ROWB, LANES)
             gg = lax.dot_general(left, right, contract, preferred_element_type=F32)
-            for px in range(SIDE):
-                rows = slice(px * EX, (px + 1) * EX)
-                total = t[py * SIDE + qy, rows, :]
-                if py > 0 and qy > 0:
-                    total = total + t[(py - 1) * SIDE + qy - 1, rows, :]
-                if py < SIDE - 1 and qy < SIDE - 1:
-                    total = total + t[(py + 1) * SIDE + qy + 1, rows, :]
-                acc = acc + gg[rows, :] * total
-    folded = acc[:, :LANES] + acc[:, LANES:]
-    folded = folded + pltpu.roll(folded, 64, 1)
-    folded = folded + pltpu.roll(folded, 32, 1)
-    folded = jnp.where(lax.axis_index("rows") == 1, pltpu.roll(folded, 16, 1), folded)
-    block_id = lax.broadcasted_iota(jnp.int32, (8, LANES), 1) // EX
-    packed = folded[0:8]
-    for j in range(1, 4):
-        packed = jnp.where(block_id == j, folded[8 * j:8 * j + 8], packed)
+            for qy in range(start, stop):
+                for px in range(SIDE):
+                    rows = slice(px * EX, (px + 1) * EX)
+                    total = t[py, rows, qy * COLB:(qy + 1) * COLB]
+                    if py > 0 and qy > 0:
+                        total = total + t[py - 1, rows, (qy - 1) * COLB:qy * COLB]
+                    if py < SIDE - 1 and qy < SIDE - 1:
+                        total = total + t[py + 1, rows, (qy + 1) * COLB:(qy + 2) * COLB]
+                    acc = acc + gg[rows, (qy - start) * COLB:(qy - start + 1) * COLB] * total
+    acc = acc + pltpu.roll(acc, 64, 1)
+    acc = acc + pltpu.roll(acc, 32, 1)
+    return acc + pltpu.roll(acc, 16, 1)
+
+
+def own_kernel(x, g, xp, gp, out_ref, lx, rx, rg, t):
+    out_ref[...] = panel_terms(x, g, xp, gp, lx, rx, rg, t)
+
+
+def cross_kernel(x, g, xp, gp, own_ref, out_ref, lx, rx, rg, t):
+    across = panel_terms(x, g, xp, gp, lx, rx, rg, t)
+    lane = lax.broadcasted_iota(jnp.int32, (8, LANES), 1)
+    is_own = (lane // PIV_DEV) % 2 == lax.axis_index("rows")
+    packed = jnp.zeros((8, LANES), F32)
+    for j in range(4):
+        rows = slice(8 * j, 8 * j + 8)
+        packed = jnp.where(lane // EX == j, jnp.where(is_own, own_ref[rows, :], across[rows]), packed)
     out_ref[...] = packed
 
 
-def main(arrays):
+def terms(kernel, arrays, shape, name):
     vmem = pl.BlockSpec(memory_space=pltpu.VMEM)
     rows, cols = SIDE * ROWB, SIDE * COLB
     return pl.pallas_call(
-        main_kernel,
-        out_shape=jax.ShapeDtypeStruct((8, LANES), F32),
-        in_specs=[vmem] * 16,
+        kernel,
+        out_shape=jax.ShapeDtypeStruct(shape, F32),
+        in_specs=[vmem] * len(arrays),
         out_specs=vmem,
         scratch_shapes=[
             pltpu.VMEM((rows, 3 * LANES), BF16),
             pltpu.VMEM((cols, 3 * LANES), BF16),
-            pltpu.VMEM((rows, LANES), BF16),
             pltpu.VMEM((cols, LANES), BF16),
-            pltpu.VMEM((SIDE * SIDE, ROWB, COLB), F32),
+            pltpu.VMEM((SIDE, ROWB, cols), F32),
         ],
-        compiler_params=pltpu.CompilerParams(vmem_limit_bytes=40 << 20),
-        name="terms",
+        compiler_params=pltpu.CompilerParams(vmem_limit_bytes=24 << 20),
+        cost_estimate=cost(2 * rows * cols * 4 * LANES, 8 << 20),
+        name=name,
     )(*arrays)
 
 
@@ -223,22 +237,25 @@
     return lax.ppermute(value, "chan", [(i, i ^ flip) for i in range(count)])
 
 
-def exchange_across(value, count, flip):
-    pairs = [(g * count + i, (1 - g) * count + (i ^ flip)) for g in range(2) for i in range(count)]
+def exchange_across(value, count):
+    pairs = [(g * count + i, (1 - g) * count + i) for g in range(2) for i in range(count)]
     return lax.ppermute(value, ("rows", "chan"), pairs)
 
 
 def local_packed(count, activations, cotangents, ordering, ridge):
     near, far = (1, 2, 3), (4, 8, 12)
     x = jnp.transpose(activations, (1, 2, 0, 3)).reshape(SIDE * SIDE, EX, CH)
-    xo, go, xp, gp = prep(ordering, x, cotangents)
+    xo, go = prep(ordering, x, cotangents)
     own_g = [go] + [exchange(go, count, f) for f in far]
-    other_g = [exchange_across(gp, count, f) for f in (0,) + far]
     own_x = [xo] + [exchange(xo, count, f) for f in near]
-    other_x = [exchange_across(xp, count, f) for f in (0,) + near]
-    term = main(own_x + other_x + own_g + other_g)
-    terms = lax.all_to_all(jnp.broadcast_to(term, (2 * count, 8, LANES)), ("rows", "chan"), 0, 0)
-    return final(terms, ridge)
+    x_all, x_piv = unpack(own_x, "unpack_x")
+    x_cross = exchange_across(x_piv, count)
+    g_all, g_piv = unpack(own_g, "unpack_g")
+    g_cross = exchange_across(g_piv, count)
+    own_term = terms(own_kernel, (x_all, g_all, x_piv, g_piv), (EX, LANES), "terms_own")
+    term = terms(cross_kernel, (x_all, g_all, x_cross, g_cross, own_term), (8, LANES), "terms_cross")
+    gathered = lax.all_to_all(jnp.broadcast_to(term, (2 * count, 8, LANES)), ("rows", "chan"), 0, 0)
+    return final(gathered, ridge)
 
 
 def jacobian_block(grad_rows, input_rows):

time: 57.2 us -> 51.9 us (0.907)
  starting transfers between devices: 20.3 us -> 12.2 us
  waiting for transfers between devices: 9.85 us -> 2.74 us
  local copies, waits for them, and re-layouts: 2.61 us -> 8.05 us
  Pallas kernels: 11 us -> 16 us
  blocking collectives: 12.5 us -> 11.8 us
    ppermute x8 -> x2, starting transfers between devices: 13.3 us -> 3.78 us  [exchange_across(): return lax.ppermute(value, ('rows', 'chan'), pairs)]
    unnamed x6 -> x30, local copies, waits for them, and re-layouts: 2.6 us -> 8.03 us
    ppermute x6, waiting for transfers between devices: 7.82 us -> 2.73 us  [exchange(): return lax.ppermute(value, 'chan', [(i, i ^ flip) for i in range(count)])]
    pallas_call x2 -> x5, Pallas kernels: 6.72 us -> 11.7 us  [the longest x2 6.03 us: terms(): pl.pallas_call(kernel, out_shape=jax.ShapeDtypeStruct(shape, F32), in_spe...]
    ppermute x8 -> x2, waiting for transfers between devices: 2.03 us -> 0.01 us  [exchange_across(): return lax.ppermute(value, ('rows', 'chan'), pairs)]
    ppermute x6, starting transfers between devices: 7.03 us -> 8.45 us  [exchange(): return lax.ppermute(value, 'chan', [(i, i ^ flip) for i in range(count)])]
    all_to_all x1, blocking collectives: 12.5 us -> 11.8 us  [local_packed(): lax.all_to_all(jnp.broadcast_to(term, (2 * count, 8, LANES)), ('rows', 'c...]
  transfers between devices with their start and end apart: 14 -> 8, of which waited for: 4 -> 2; matrix products, arithmetic and copies ran while one was open for 0% -> 0% of each run, Pallas kernels for 0% -> 15%
where the time goes in v3:
time: 51.9 us; the launch traced here: 51.5 us
  Pallas kernels  16 us (31%)
  starting transfers between devices  12.2 us (24%)
  blocking collectives  11.8 us (23%)
  local copies, waits for them, and re-layouts  8.05 us (16%)
  waiting for transfers between devices  2.74 us (5%)
  between operations  0.71 us (1%)
    all_to_all x1, blocking collectives, local_packed(): lax.all_to_all(jnp.broadcast_to(term, (2 * count, 8, LANES)), ('rows', 'c...  11.8 us
    ppermute x6, starting transfers between devices, exchange(): return lax.ppermute(value, 'chan', [(i, i ^ flip) for i in range(count)])  8.45 us
    unnamed x30, local copies, waits for them, and re-layouts  8.03 us
    pallas_call x2, Pallas kernels, terms(): pl.pallas_call(kernel, out_shape=jax.ShapeDtypeStruct(shape, F32), in_spe...  6.03 us
    pallas_call x2, Pallas kernels, unpack(): pl.pallas_call(unpack_kernel, out_shape=(jax.ShapeDtypeStruct((SPOTS, EX,...  4.53 us
    pallas_call x1, Pallas kernels, final(): pl.pallas_call(final_kernel, out_shape=(out, out), in_specs=[vmem] * 2, o...  4.3 us
    ppermute x2, starting transfers between devices, exchange_across(): return lax.ppermute(value, ('rows', 'chan'), pairs)  3.78 us
    ppermute x6, waiting for transfers between devices, exchange(): return lax.ppermute(value, 'chan', [(i, i ^ flip) for i in range(count)])  2.73 us
  transfers between devices with their start and end apart: 8, of which 2 were waited for; matrix products, arithmetic and copies ran while one was open for 0% of the time, Pallas kernels for 15%

profile of v3, /device:TPU:0, one launch (start us, length us, event | category | flops | bytes accessed | tf_op | source)
XLA Modules:
  0.0 51.5 jit_solution(9255296340341062778)
XLA Ops:
  0.6 0.6 %copy-done.4 = s32[1,32]{1,0:T(1,128)S(1)} copy-done((s32[1,32]{1,0:T(1,128)S(1)}, s32[1,32]{1,0:T(1,128)}, u32[]{:S(2)}) %copy-start.4) | copy-done | bytes 152
  1.3 1.0 %copy-done = bf16[32,7,7,32]{3,0,2,1:T(8,128)(2,1)S(1)} copy-done((bf16[32,7,7,32]{3,0,2,1:T(8,128)(2,1)S(1)}, bf16[32,7,7,32]{3,0,2,1:T(8,128)(2,1)}, u32[]{:S(2)}) %copy-start) | copy-done | bytes 100376
  2.3 0.9 %copy-done.1 = bf16[32,32,49]{2,1,0:T(8,128)(2,1)S(1)} copy-done((bf16[32,32,49]{2,1,0:T(8,128)(2,1)S(1)}, bf16[32,32,49]{2,1,0:T(8,128)(2,1)}, u32[]{:S(2)}) %copy-start.1) | copy-done | bytes 100376
  3.2 1.1 %prep.1 = (bf16[14,32,128]{2,1,0:T(8,128)(2,1)S(1)}, bf16[14,32,128]{2,1,0:T(8,128)(2,1)S(1)}) custom-call(s32[1,32]{1,0:T(1,128)S(1)} %copy-done.4, bf16[49,32,32]{2,1,0:T(8,128)(2,1)S(1)} %bitcast.4, bf16[32,32,49]{2,1,0:T(8,128)(2,1)S(1)} %copy-done.1), custom_call_target="tpu_custom_call" | custom-call | tf_op jit(solution)/shard_map/prep/pallas_call | solution.py:60
  4.4 2.5 %collective-permute-start.2 = (bf16[14,32,128]{2,1,0:T(8,128)(2,1)S(1)}, bf16[14,32,128]{2,1,0:T(8,128)(2,1)S(1)}, u32[]{:S(2)}, u32[]{:S(2)}) collective-permute-start(bf16[14,32,128]{2,1,0:T(8,128)(2,1)S(1)} %get-tuple-element.8.refs_0_), channel_id=1, source_target_pairs={{0,3},{1,2},{2,1},{3,0},{4,7},{5,6},{6,5},{7,4},{8,11},{9,10},{10,... | collective-permute-start | bytes 344072 | tf_op jit(solution)/shard_map/ppermute | solution.py:237
  6.9 0.6 %collective-permute-start.1 = (bf16[14,32,128]{2,1,0:T(8,128)(2,1)S(1)}, bf16[14,32,128]{2,1,0:T(8,128)(2,1)S(1)}, u32[]{:S(2)}, u32[]{:S(2)}) collective-permute-start(bf16[14,32,128]{2,1,0:T(8,128)(2,1)S(1)} %get-tuple-element.8.refs_0_), channel_id=1, source_target_pairs={{0,2},{1,3},{2,0},{3,1},{4,6},{5,7},{6,4},{7,5},{8,10},{9,11},{10,... | collective-permute-start | bytes 344072 | tf_op jit(solution)/shard_map/ppermute | solution.py:237
  7.5 3.8 %collective-permute-start.5 = (bf16[14,32,128]{2,1,0:T(8,128)(2,1)S(1)}, bf16[14,32,128]{2,1,0:T(8,128)(2,1)S(1)}, u32[]{:S(2)}, u32[]{:S(2)}) collective-permute-start(bf16[14,32,128]{2,1,0:T(8,128)(2,1)S(1)} %get-tuple-element.10.refs_0_), channel_id=1, source_target_pairs={{0,12},{1,13},{2,14},{3,15},{4,8},{5,9},{6,10},{7,11},{8,4},{9,5},... | collective-permute-start | bytes 344072 | tf_op jit(solution)/shard_map/ppermute | solution.py:237
  11.4 1.5 %collective-permute-start.3 = (bf16[14,32,128]{2,1,0:T(8,128)(2,1)S(1)}, bf16[14,32,128]{2,1,0:T(8,128)(2,1)S(1)}, u32[]{:S(2)}, u32[]{:S(2)}) collective-permute-start(bf16[14,32,128]{2,1,0:T(8,128)(2,1)S(1)} %get-tuple-element.10.refs_0_), channel_id=1, source_target_pairs={{0,4},{1,5},{2,6},{3,7},{4,0},{5,1},{6,2},{7,3},{8,12},{9,13},{10,... | collective-permute-start | bytes 344072 | tf_op jit(solution)/shard_map/ppermute | solution.py:237
  13.0 0.6 %copy-done.13 = bf16[14,32,128]{2,1,0:T(8,128)(2,1)} copy-done((bf16[14,32,128]{2,1,0:T(8,128)(2,1)}, bf16[14,32,128]{2,1,0:T(8,128)(2,1)S(1)}, u32[]{:S(2)}) %copy-start.13) | copy-done | bytes 114712
  13.7 0.6 %copy-done.14 = bf16[14,32,128]{2,1,0:T(8,128)(2,1)} copy-done((bf16[14,32,128]{2,1,0:T(8,128)(2,1)}, bf16[14,32,128]{2,1,0:T(8,128)(2,1)S(1)}, u32[]{:S(2)}) %copy-start.14) | copy-done | bytes 114712
  14.3 2.3 %unpack_x.1 = (bf16[49,32,128]{2,1,0:T(8,128)(2,1)}, bf16[49,16,128]{2,1,0:T(8,128)(2,1)}) custom-call(bf16[14,32,128]{2,1,0:T(8,128)(2,1)} %copy-done.3, bf16[14,32,128]{2,1,0:T(8,128)(2,1)} %copy-done.14, bf16[14,32,128]{2,1,0:T(8,128)(2,1)} %copy-done.13, bf16[14,32,128]{2,1,0:T(8,128)(2,1)} %copy-done.11), custom_call_target="tpu_custom_call" | custom-call | bytes 1048576 | tf_op jit(solution)/shard_map/unpack_x/pallas_call | solution.py:99
  16.6 2.3 %collective-permute-start.6 = (bf16[49,16,128]{2,1,0:T(8,128)(2,1)}, bf16[49,16,128]{2,1,0:T(8,128)(2,1)S(1)}, u32[]{:S(2)}, u32[]{:S(2)}) collective-permute-start(bf16[49,16,128]{2,1,0:T(8,128)(2,1)} %get-tuple-element.12.xp), channel_id=1, source_target_pairs={{0,16},{1,17},{2,18},{3,19},{4,20},{5,21},{6,22},{7,23},{8,24},{9,... | collective-permute-start | bytes 602120 | tf_op jit(solution)/shard_map/ppermute | solution.py:242
  18.9 2.5 %collective-permute-done.4.refs_2_ = bf16[14,32,128]{2,1,0:T(8,128)(2,1)S(1)} collective-permute-done((bf16[14,32,128]{2,1,0:T(8,128)(2,1)S(1)}, bf16[14,32,128]{2,1,0:T(8,128)(2,1)S(1)}, u32[]{:S(2)}, u32[]{:S(2)}) %collective-permute-start.4) | collective-permute-done | bytes 114720 | tf_op jit(solution)/shard_map/ppermute | solution.py:237
  21.5 0.6 %copy-done.10 = bf16[14,32,128]{2,1,0:T(8,128)(2,1)} copy-done((bf16[14,32,128]{2,1,0:T(8,128)(2,1)}, bf16[14,32,128]{2,1,0:T(8,128)(2,1)S(1)}, u32[]{:S(2)}) %copy-start.10) | copy-done | bytes 114712
  22.1 0.6 %copy-done.12 = bf16[14,32,128]{2,1,0:T(8,128)(2,1)} copy-done((bf16[14,32,128]{2,1,0:T(8,128)(2,1)}, bf16[14,32,128]{2,1,0:T(8,128)(2,1)S(1)}, u32[]{:S(2)}) %copy-start.12) | copy-done | bytes 114712
  22.7 2.3 %unpack_g.1 = (bf16[49,32,128]{2,1,0:T(8,128)(2,1)}, bf16[49,16,128]{2,1,0:T(8,128)(2,1)}) custom-call(bf16[14,32,128]{2,1,0:T(8,128)(2,1)} %copy-done.2, bf16[14,32,128]{2,1,0:T(8,128)(2,1)} %copy-done.12, bf16[14,32,128]{2,1,0:T(8,128)(2,1)} %copy-done.10, bf16[14,32,128]{2,1,0:T(8,128)(2,1)} %copy-done.9), custom_call_target="tpu_custom_call" | custom-call | bytes 1048576 | tf_op jit(solution)/shard_map/unpack_g/pallas_call | solution.py:99
  25.0 1.5 %collective-permute-start.7 = (bf16[49,16,128]{2,1,0:T(8,128)(2,1)}, bf16[49,16,128]{2,1,0:T(8,128)(2,1)S(1)}, u32[]{:S(2)}, u32[]{:S(2)}) collective-permute-start(bf16[49,16,128]{2,1,0:T(8,128)(2,1)} %get-tuple-element.13.gp), channel_id=1, source_target_pairs={{0,16},{1,17},{2,18},{3,19},{4,20},{5,21},{6,22},{7,23},{8,24},{9,... | collective-permute-start | bytes 602120 | tf_op jit(solution)/shard_map/ppermute | solution.py:242
  26.5 1.0 %copy-done.6 = bf16[49,32,128]{2,1,0:T(8,128)(2,1)S(1)} copy-done((bf16[49,32,128]{2,1,0:T(8,128)(2,1)S(1)}, bf16[49,32,128]{2,1,0:T(8,128)(2,1)}, u32[]{:S(2)}) %copy-start.6) | copy-done | bytes 401432
  27.5 0.9 %copy-done.7 = bf16[49,16,128]{2,1,0:T(8,128)(2,1)S(1)} copy-done((bf16[49,16,128]{2,1,0:T(8,128)(2,1)S(1)}, bf16[49,16,128]{2,1,0:T(8,128)(2,1)}, u32[]{:S(2)}) %copy-start.7) | copy-done | bytes 200728
  28.4 0.9 %copy-done.8 = bf16[49,16,128]{2,1,0:T(8,128)(2,1)S(1)} copy-done((bf16[49,16,128]{2,1,0:T(8,128)(2,1)S(1)}, bf16[49,16,128]{2,1,0:T(8,128)(2,1)}, u32[]{:S(2)}) %copy-start.8) | copy-done | bytes 200728
  29.4 3.0 %terms_own.1.own_ref = f32[32,128]{1,0:T(8,128)S(1)} custom-call(bf16[49,32,128]{2,1,0:T(8,128)(2,1)S(1)} %copy-done.5, bf16[49,32,128]{2,1,0:T(8,128)(2,1)S(1)} %copy-done.6, bf16[49,16,128]{2,1,0:T(8,128)(2,1)S(1)} %copy-done.7, bf16[49,16,128]{2,1,0:T(8,128)(2,1)S(1)} %copy-done.8), custom_call_target="tpu_custom_call" | custom-call | flops 1438646272 | bytes 8388608 | tf_op jit(solution)/shard_map/terms_own/pallas_call | solution.py:171
  32.4 3.0 %terms_cross.1 = f32[8,128]{1,0:T(8,128)S(1)} custom-call(bf16[49,32,128]{2,1,0:T(8,128)(2,1)S(1)} %copy-done.5, bf16[49,32,128]{2,1,0:T(8,128)(2,1)S(1)} %copy-done.6, bf16[49,16,128]{2,1,0:T(8,128)(2,1)S(1)} %collective-permute-done.6.xp, bf16[49,16,128]{2,1,0:T(8,128)(2,1)S(1)} %collective-permute-done.7.gp, f32[32,128]{1,0:T(8,128)S(1)} %terms_own.1.own_ref), custom_call_target="tpu_custom_call" | custom-call | flops 1438646272 | bytes 8388608 | tf_op jit(solution)/shard_map/terms_cross/pallas_call | solution.py:171
  35.4 11.8 %all_to_all.5.terms_ref = f32[32,8,128]{2,1,0:T(8,128)} all-to-all(f32[32,8,128]{2,1,0:T(8,128)S(1)} %broadcast_in_dim.3), channel_id=1, replica_groups=mesh['rows'=2,'chan'=16] {'rows','chan'}, dimensions={0} | all-to-all | bytes 262144 | tf_op jit(solution)/shard_map/all_to_all | solution.py:257
  47.2 4.3 %solve.1 = (f32[32,32]{1,0:T(8,128)}, f32[32,32]{1,0:T(8,128)}) custom-call(f32[32,8,128]{2,1,0:T(8,128)} %all_to_all.5.terms_ref, f32[1,32]{1,0:T(1,128)} %bitcast.5), custom_call_target="tpu_custom_call" | custom-call | tf_op jit(solution)/shard_map/solve/pallas_call | solution.py:227
  (30 shorter events, 0.3 us)
Async XLA Ops:
  0.6 0.7 %copy-start.4 = (s32[1,32]{1,0:T(1,128)S(1)}, s32[1,32]{1,0:T(1,128)}, u32[]{:S(2)}) copy-start(s32[1,32]{1,0:T(1,128)} %order_ref.1) | copy-start | bytes 388
  1.3 1.0 %copy-start = (bf16[32,7,7,32]{3,0,2,1:T(8,128)(2,1)S(1)}, bf16[32,7,7,32]{3,0,2,1:T(8,128)(2,1)}, u32[]{:S(2)}) copy-start(bf16[32,7,7,32]{3,0,2,1:T(8,128)(2,1)} %param.4) | copy-start | bytes 301060
  2.3 0.9 %copy-start.1 = (bf16[32,32,49]{2,1,0:T(8,128)(2,1)S(1)}, bf16[32,32,49]{2,1,0:T(8,128)(2,1)}, u32[]{:S(2)}) copy-start(bf16[32,32,49]{2,1,0:T(8,128)(2,1)} %g_ref.1) | copy-start | bytes 301060
  4.4 8.7 %copy-start.3 = (bf16[14,32,128]{2,1,0:T(8,128)(2,1)}, bf16[14,32,128]{2,1,0:T(8,128)(2,1)S(1)}, u32[]{:S(2)}) copy-start(bf16[14,32,128]{2,1,0:T(8,128)(2,1)S(1)} %get-tuple-element.8.refs_0_) | copy-start | bytes 344068
  4.4 12.2 %copy-start.2 = (bf16[14,32,128]{2,1,0:T(8,128)(2,1)}, bf16[14,32,128]{2,1,0:T(8,128)(2,1)S(1)}, u32[]{:S(2)}) copy-start(bf16[14,32,128]{2,1,0:T(8,128)(2,1)S(1)} %get-tuple-element.10.refs_0_) | copy-start | bytes 344068
  4.4 7.0 %collective-permute-start.2 = (bf16[14,32,128]{2,1,0:T(8,128)(2,1)S(1)}, bf16[14,32,128]{2,1,0:T(8,128)(2,1)S(1)}, u32[]{:S(2)}, u32[]{:S(2)}) collective-permute-start(bf16[14,32,128]{2,1,0:T(8,128)(2,1)S(1)} %get-tuple-element.8.refs_0_), channel_id=1, source_target_pairs={{0,3},{1,2},{2,1},{3,0},{4,7},{5,6},{6,5},{7,4},{8,11},{9,10},{10,... | collective-permute-start | bytes 344072 | tf_op jit(solution)/shard_map/ppermute | solution.py:237
  6.9 6.2 %collective-permute-start.1 = (bf16[14,32,128]{2,1,0:T(8,128)(2,1)S(1)}, bf16[14,32,128]{2,1,0:T(8,128)(2,1)S(1)}, u32[]{:S(2)}, u32[]{:S(2)}) collective-permute-start(bf16[14,32,128]{2,1,0:T(8,128)(2,1)S(1)} %get-tuple-element.8.refs_0_), channel_id=1, source_target_pairs={{0,2},{1,3},{2,0},{3,1},{4,6},{5,7},{6,4},{7,5},{8,10},{9,11},{10,... | collective-permute-start | bytes 344072 | tf_op jit(solution)/shard_map/ppermute | solution.py:237
  7.5 5.5 %collective-permute-start = (bf16[14,32,128]{2,1,0:T(8,128)(2,1)S(1)}, bf16[14,32,128]{2,1,0:T(8,128)(2,1)S(1)}, u32[]{:S(2)}, u32[]{:S(2)}) collective-permute-start(bf16[14,32,128]{2,1,0:T(8,128)(2,1)S(1)} %get-tuple-element.8.refs_0_), channel_id=1, source_target_pairs={{0,1},{1,0},{2,3},{3,2},{4,5},{5,4},{6,7},{7,6},{8,9},{9,8},{10,11... | collective-permute-start | bytes 344072 | tf_op jit(solution)/shard_map/ppermute | solution.py:237
  7.5 11.4 %collective-permute-start.5 = (bf16[14,32,128]{2,1,0:T(8,128)(2,1)S(1)}, bf16[14,32,128]{2,1,0:T(8,128)(2,1)S(1)}, u32[]{:S(2)}, u32[]{:S(2)}) collective-permute-start(bf16[14,32,128]{2,1,0:T(8,128)(2,1)S(1)} %get-tuple-element.10.refs_0_), channel_id=1, source_target_pairs={{0,12},{1,13},{2,14},{3,15},{4,8},{5,9},{6,10},{7,11},{8,4},{9,5},... | collective-permute-start | bytes 344072 | tf_op jit(solution)/shard_map/ppermute | solution.py:237
  11.4 10.1 %collective-permute-start.4 = (bf16[14,32,128]{2,1,0:T(8,128)(2,1)S(1)}, bf16[14,32,128]{2,1,0:T(8,128)(2,1)S(1)}, u32[]{:S(2)}, u32[]{:S(2)}) collective-permute-start(bf16[14,32,128]{2,1,0:T(8,128)(2,1)S(1)} %get-tuple-element.10.refs_0_), channel_id=1, source_target_pairs={{0,8},{1,9},{2,10},{3,11},{4,12},{5,13},{6,14},{7,15},{8,0},{9,1},... | collective-permute-start | bytes 344072 | tf_op jit(solution)/shard_map/ppermute | solution.py:237
  11.4 1.7 %copy-start.11 = (bf16[14,32,128]{2,1,0:T(8,128)(2,1)}, bf16[14,32,128]{2,1,0:T(8,128)(2,1)S(1)}, u32[]{:S(2)}) copy-start(bf16[14,32,128]{2,1,0:T(8,128)(2,1)S(1)} %collective-permute-done.2.refs_3_) | copy-start | bytes 344068
  11.4 10.1 %collective-permute-start.3 = (bf16[14,32,128]{2,1,0:T(8,128)(2,1)S(1)}, bf16[14,32,128]{2,1,0:T(8,128)(2,1)S(1)}, u32[]{:S(2)}, u32[]{:S(2)}) collective-permute-start(bf16[14,32,128]{2,1,0:T(8,128)(2,1)S(1)} %get-tuple-element.10.refs_0_), channel_id=1, source_target_pairs={{0,4},{1,5},{2,6},{3,7},{4,0},{5,1},{6,2},{7,3},{8,12},{9,13},{10,... | collective-permute-start | bytes 344072 | tf_op jit(solution)/shard_map/ppermute | solution.py:237
  13.0 0.7 %copy-start.13 = (bf16[14,32,128]{2,1,0:T(8,128)(2,1)}, bf16[14,32,128]{2,1,0:T(8,128)(2,1)S(1)}, u32[]{:S(2)}) copy-start(bf16[14,32,128]{2,1,0:T(8,128)(2,1)S(1)} %collective-permute-done.1.refs_2_) | copy-start | bytes 344068
  13.7 0.6 %copy-start.14 = (bf16[14,32,128]{2,1,0:T(8,128)(2,1)}, bf16[14,32,128]{2,1,0:T(8,128)(2,1)S(1)}, u32[]{:S(2)}) copy-start(bf16[14,32,128]{2,1,0:T(8,128)(2,1)S(1)} %collective-permute-done.refs_1_) | copy-start | bytes 344068
  16.6 9.9 %copy-start.5 = (bf16[49,32,128]{2,1,0:T(8,128)(2,1)S(1)}, bf16[49,32,128]{2,1,0:T(8,128)(2,1)}, u32[]{:S(2)}) copy-start(bf16[49,32,128]{2,1,0:T(8,128)(2,1)} %get-tuple-element.9.x) | copy-start | bytes 1204228
  16.6 15.8 %collective-permute-start.6 = (bf16[49,16,128]{2,1,0:T(8,128)(2,1)}, bf16[49,16,128]{2,1,0:T(8,128)(2,1)S(1)}, u32[]{:S(2)}, u32[]{:S(2)}) collective-permute-start(bf16[49,16,128]{2,1,0:T(8,128)(2,1)} %get-tuple-element.12.xp), channel_id=1, source_target_pairs={{0,16},{1,17},{2,18},{3,19},{4,20},{5,21},{6,22},{7,23},{8,24},{9,... | collective-permute-start | bytes 602120 | tf_op jit(solution)/shard_map/ppermute | solution.py:242
  18.9 2.6 %copy-start.9 = (bf16[14,32,128]{2,1,0:T(8,128)(2,1)}, bf16[14,32,128]{2,1,0:T(8,128)(2,1)S(1)}, u32[]{:S(2)}) copy-start(bf16[14,32,128]{2,1,0:T(8,128)(2,1)S(1)} %collective-permute-done.5.refs_3_) | copy-start | bytes 344068
  21.4 0.7 %copy-start.10 = (bf16[14,32,128]{2,1,0:T(8,128)(2,1)}, bf16[14,32,128]{2,1,0:T(8,128)(2,1)S(1)}, u32[]{:S(2)}) copy-start(bf16[14,32,128]{2,1,0:T(8,128)(2,1)S(1)} %collective-permute-done.4.refs_2_) | copy-start | bytes 344068
  22.1 0.6 %copy-start.12 = (bf16[14,32,128]{2,1,0:T(8,128)(2,1)}, bf16[14,32,128]{2,1,0:T(8,128)(2,1)S(1)}, u32[]{:S(2)}) copy-start(bf16[14,32,128]{2,1,0:T(8,128)(2,1)S(1)} %collective-permute-done.3.refs_1_) | copy-start | bytes 344068
  25.0 7.4 %collective-permute-start.7 = (bf16[49,16,128]{2,1,0:T(8,128)(2,1)}, bf16[49,16,128]{2,1,0:T(8,128)(2,1)S(1)}, u32[]{:S(2)}, u32[]{:S(2)}) collective-permute-start(bf16[49,16,128]{2,1,0:T(8,128)(2,1)} %get-tuple-element.13.gp), channel_id=1, source_target_pairs={{0,16},{1,17},{2,18},{3,19},{4,20},{5,21},{6,22},{7,23},{8,24},{9,... | collective-permute-start | bytes 602120 | tf_op jit(solution)/shard_map/ppermute | solution.py:242
  26.5 1.0 %copy-start.6 = (bf16[49,32,128]{2,1,0:T(8,128)(2,1)S(1)}, bf16[49,32,128]{2,1,0:T(8,128)(2,1)}, u32[]{:S(2)}) copy-start(bf16[49,32,128]{2,1,0:T(8,128)(2,1)} %get-tuple-element.11.g) | copy-start | bytes 1204228
  27.5 0.9 %copy-start.7 = (bf16[49,16,128]{2,1,0:T(8,128)(2,1)S(1)}, bf16[49,16,128]{2,1,0:T(8,128)(2,1)}, u32[]{:S(2)}) copy-start(bf16[49,16,128]{2,1,0:T(8,128)(2,1)} %get-tuple-element.12.xp) | copy-start | bytes 602116
  28.4 0.9 %copy-start.8 = (bf16[49,16,128]{2,1,0:T(8,128)(2,1)S(1)}, bf16[49,16,128]{2,1,0:T(8,128)(2,1)}, u32[]{:S(2)}) copy-start(bf16[49,16,128]{2,1,0:T(8,128)(2,1)} %get-tuple-element.13.gp) | copy-start | bytes 602116
